TPU v7x, 128 devices: a whole 4x4x4 slice. The times are simulated.
128 devices in a mesh: section: 2 (over core), fsdp: 64 (over z, x, y).
Axes of the slice: x: 4, y: 4, z: 4, core: 2. Of those that a mesh axis runs over, the one named last changes fastest.
Arguments:
- tokens: bfloat16 [8192, 896], P('fsdp'), may hold values from -6 to 6
- segments: int32 [8192], P('fsdp'), may hold values from 0 to 3, as said below
- cotangent: bfloat16 [8192, 896], P('fsdp'), may hold values from -6 to 6
- w_qkv: bfloat16 [2, 896, 1152], P('section', 'fsdp'), may hold values from -0.1875 to 0.1875
- b_qkv: bfloat16 [2, 1152], P('section', 'fsdp'), may hold values from -3 to 3
- w_out: bfloat16 [2, 896, 896], P('section', 'fsdp'), may hold values from -0.75 to 0.75
- gain_attn: bfloat16 [2, 896], P('section', 'fsdp'), may hold values from 0.5 to 1.5
- gain_mlp: bfloat16 [2, 896], P('section', 'fsdp'), may hold values from 0.5 to 1.5
- w_gate: bfloat16 [2, 896, 4864], P('section', 'fsdp'), may hold values from -0.1875 to 0.1875
- w_up: bfloat16 [2, 896, 4864], P('section', 'fsdp'), may hold values from -0.1875 to 0.1875
- w_down: bfloat16 [2, 4864, 896], P('section', 'fsdp'), may hold values from -0.078125 to 0.078125
Outputs:
- states: bfloat16 [2, 8192, 896], P('section', 'fsdp')
- input_grads: float32 [2, 8192, 896], P('section', 'fsdp')
- grad_w_qkv: float32 [2, 896, 1152], P('section', 'fsdp')
- grad_b_qkv: float32 [2, 1152], P('section', 'fsdp')
- grad_w_out: float32 [2, 896, 896], P('section', 'fsdp')
- grad_gain_attn: float32 [2, 896], P('section', 'fsdp')
- grad_gain_mlp: float32 [2, 896], P('section', 'fsdp')
- grad_w_gate: float32 [2, 896, 4864], P('section', 'fsdp')
- grad_w_up: float32 [2, 896, 4864], P('section', 'fsdp')
- grad_w_down: float32 [2, 4864, 896], P('section', 'fsdp')
Inputs may be any that keep to these rules, and one draw needn't show every extreme that they name: `segments`: within each block of 64 tokens the ids start at 0 and never fall; a block holds one to four sequences, and the number differs between blocks; block 0 holds four, block 1 one.
All inputs are finite; a program needn't handle non-finite values.
Results may differ from a plain program's by a relative error of at most 0.018.
Values may be sent and summed in bfloat16 or wider, within the bound.
A program may use at most 512 MiB of HBM per device.

v0:
```python
import math

import jax
import jax.numpy as jnp
from jax import lax
from jax.sharding import PartitionSpec as P

D = 896
QH = 14
KVH = 2
HD = 64
ROWS = 64
MB = 2


eps_norm = 1e-06
theta_base = 1000000.0


def sent_together(arrays, axis, dim, along):
    widths = [math.prod(a.shape[along:]) for a in arrays]
    both = jnp.concatenate(
        [a.reshape(*a.shape[:along], w) for a, w in zip(arrays, widths)], axis=along
    )
    filled = lax.all_gather(both, axis, axis=dim, tiled=True)
    pieces = jnp.split(filled, [sum(widths[:k]) for k in range(1, len(widths))], axis=along)
    return tuple(
        (b.reshape(*filled.shape[:along], *a.shape[along:]) for a, b in zip(arrays, pieces))
    )


def shifted(block, axis, distance):
    devices = range(lax.axis_size(axis))
    route = [(i - distance, i) for i in devices if i - distance in devices]
    return lax.ppermute(block, axis, route)


def split_up(array, dim, devices):
    lengths = array.shape
    pieces = array.reshape(*lengths[:dim], devices, lengths[dim] // devices, *lengths[dim + 1 :])
    return jnp.moveaxis(pieces, dim, 0)


def sum_packed(arrays, axis, dims):
    devices = lax.axis_size(axis)
    pieces = [split_up(a, dim, devices) for a, dim in zip(arrays, dims)]
    lines = jnp.concatenate([b.reshape(devices, -1) for b in pieces], axis=1)
    span = max(16, -(-lines.shape[1] // 1024) * 8)
    lines = jnp.pad(lines, ((0, 0), (0, span * 128 - lines.shape[1]))).reshape(-1, 128)
    flat, at, finished = (lax.psum_scatter(lines, axis, tiled=True).reshape(-1), 0, [])
    for b in pieces:
        part = b[0]
        finished.append(flat[at : at + part.size].reshape(part.shape))
        at += part.size
    return tuple(finished)


def rotation(segment):
    index = jnp.arange(segment.shape[0], dtype=jnp.int32)
    earlier = jnp.sum((segment[None, :] < segment[:, None]).astype(jnp.int32), axis=1)
    place = (index - earlier).astype(jnp.float32)
    half = HD // 2
    inverse = theta_base ** (-(jnp.arange(half, dtype=jnp.float32) * 2.0 / HD))
    angles = place[:, None] * inverse[None, :]
    return (jnp.cos(angles), jnp.sin(angles))


def rotate(values, cosine, sine):
    half = HD // 2
    first = values[..., :half]
    second = values[..., half:]
    cosine = cosine[:, None, :]
    sine = sine[:, None, :]
    return jnp.concatenate(
        [first * cosine - second * sine, second * cosine + first * sine], axis=-1
    )


def unrotate(values, cosine, sine):
    half = HD // 2
    first = values[..., :half]
    second = values[..., half:]
    cosine = cosine[:, None, :]
    sine = sine[:, None, :]
    return jnp.concatenate(
        [first * cosine + second * sine, second * cosine - first * sine], axis=-1
    )


def back_product(left, right):
    return lax.dot_general(
        left, right, (((1,), (1,)), ((), ())), preferred_element_type=jnp.float32
    )


def row_product(left, right):
    return lax.dot_general(
        left, right, (((0,), (0,)), ((), ())), preferred_element_type=jnp.float32
    )


def allowed_mask(segment):
    index = jnp.arange(segment.shape[0])
    return (segment[:, None] == segment[None, :]) & (index[None, :] <= index[:, None])


def masked_scores(queries, keys, segment):
    rows = queries.shape[0]
    grouped = queries.reshape(rows, KVH, QH // KVH, HD)
    scores = jnp.einsum(
        "rkgd,skd->kgrs", grouped, keys, preferred_element_type=jnp.float32
    ) * HD ** (-0.5)
    return (jnp.where(allowed_mask(segment), scores, -1e30), grouped)


def layer_ahead(params, stream_in, segment):
    w_qkv, b_qkv, w_out, gain_attn, gain_mlp, w_gate, w_up, w_down = params
    rows = stream_in.shape[0]
    stream = stream_in.astype(jnp.float32)
    inverse_one = lax.rsqrt(jnp.mean(stream * stream, axis=-1, keepdims=True) + eps_norm)
    unit_one = stream * inverse_one
    normed = (unit_one * gain_attn.astype(jnp.float32)).astype(jnp.bfloat16)
    projected = jnp.dot(normed, w_qkv, preferred_element_type=jnp.float32) + b_qkv.astype(
        jnp.float32
    )
    cosine, sine = rotation(segment)
    queries = rotate(projected[:, : QH * HD].reshape(rows, QH, HD), cosine, sine).astype(
        jnp.bfloat16
    )
    keys = rotate(
        projected[:, QH * HD : QH * HD + KVH * HD].reshape(rows, KVH, HD), cosine, sine
    ).astype(jnp.bfloat16)
    values = projected[:, QH * HD + KVH * HD :].reshape(rows, KVH, HD).astype(jnp.bfloat16)
    masked, grouped = masked_scores(queries, keys, segment)
    top = jnp.max(masked, axis=-1, keepdims=True)
    weights = jnp.exp(masked - top)
    totals = jnp.sum(weights, axis=-1, keepdims=True)
    probs = (weights / totals).astype(jnp.bfloat16)
    log_total = top + jnp.log(totals)
    mixed = jnp.einsum("kgrs,skd->rkgd", probs, values, preferred_element_type=jnp.float32)
    mixed = mixed.reshape(rows, QH * HD).astype(jnp.bfloat16)
    middle = stream + jnp.dot(mixed, w_out, preferred_element_type=jnp.float32)
    inverse_two = lax.rsqrt(jnp.mean(middle * middle, axis=-1, keepdims=True) + eps_norm)
    unit_two = middle * inverse_two
    normed_mlp = (unit_two * gain_mlp.astype(jnp.float32)).astype(jnp.bfloat16)
    gate = jnp.dot(normed_mlp, w_gate, preferred_element_type=jnp.float32)
    upward = jnp.dot(normed_mlp, w_up, preferred_element_type=jnp.float32)
    active = (jax.nn.silu(gate) * upward).astype(jnp.bfloat16)
    output = middle + jnp.dot(active, w_down, preferred_element_type=jnp.float32)
    cache = (
        inverse_one,
        unit_one,
        normed,
        queries,
        keys,
        values,
        log_total,
        mixed,
        inverse_two,
        unit_two,
        normed_mlp,
        gate,
        upward,
        active,
    )
    return (output, cache)


def norm_back(grad_unit, unit, inverse):
    return inverse * (grad_unit - unit * jnp.mean(grad_unit * unit, axis=-1, keepdims=True))


def layer_back(params, cache, grad_out, segment):
    w_qkv, b_qkv, w_out, gain_attn, gain_mlp, w_gate, w_up, w_down = params
    (
        inverse_one,
        unit_one,
        normed,
        queries,
        keys,
        values,
        log_total,
        mixed,
        inverse_two,
        unit_two,
        normed_mlp,
        gate,
        upward,
        active,
    ) = cache
    rows = grad_out.shape[0]
    grad_down_in = grad_out.astype(jnp.bfloat16)
    grad_active = back_product(grad_down_in, w_down)
    sigmoid_gate = jax.nn.sigmoid(gate)
    grad_gate = (
        grad_active * upward * (sigmoid_gate * (1.0 + gate * (1.0 - sigmoid_gate)))
    ).astype(jnp.bfloat16)
    grad_upward = (grad_active * gate * sigmoid_gate).astype(jnp.bfloat16)
    grad_normed_mlp = back_product(grad_gate, w_gate) + back_product(grad_upward, w_up)
    gain_two_grad = jnp.sum(grad_normed_mlp * unit_two, axis=0)
    grad_middle = grad_out + norm_back(
        grad_normed_mlp * gain_mlp.astype(jnp.float32), unit_two, inverse_two
    )
    grad_attended = grad_middle.astype(jnp.bfloat16)
    grad_mixed = (
        back_product(grad_attended, w_out).astype(jnp.bfloat16).reshape(rows, KVH, QH // KVH, HD)
    )
    masked, grouped = masked_scores(queries, keys, segment)
    probs = jnp.exp(masked - log_total)
    grad_probs = jnp.einsum(
        "rkgd,skd->kgrs", grad_mixed, values, preferred_element_type=jnp.float32
    )
    grad_values = jnp.einsum(
        "kgrs,rkgd->skd", probs.astype(jnp.bfloat16), grad_mixed, preferred_element_type=jnp.float32
    )
    grad_scores = (
        probs * (grad_probs - jnp.sum(grad_probs * probs, axis=-1, keepdims=True))
    ).astype(jnp.bfloat16)
    grad_queries = jnp.einsum(
        "kgrs,skd->rkgd", grad_scores, keys, preferred_element_type=jnp.float32
    ) * HD ** (-0.5)
    grad_keys = jnp.einsum(
        "kgrs,rkgd->skd", grad_scores, grouped, preferred_element_type=jnp.float32
    ) * HD ** (-0.5)
    cosine, sine = rotation(segment)
    grad_queries = unrotate(grad_queries.reshape(rows, QH, HD), cosine, sine).reshape(rows, QH * HD)
    grad_keys = unrotate(grad_keys, cosine, sine).reshape(rows, KVH * HD)
    grad_projected = jnp.concatenate(
        [grad_queries, grad_keys, grad_values.reshape(rows, KVH * HD)], axis=1
    )
    grad_projected = grad_projected.astype(jnp.bfloat16)
    grad_normed = back_product(grad_projected, w_qkv)
    gain_one_grad = jnp.sum(grad_normed * unit_one, axis=0)
    grad_input = grad_middle + norm_back(
        grad_normed * gain_attn.astype(jnp.float32), unit_one, inverse_one
    )
    terms = (
        row_product(normed, grad_projected),
        jnp.sum(grad_projected.astype(jnp.float32), axis=0),
        row_product(mixed, grad_attended),
        gain_one_grad,
        gain_two_grad,
        row_product(normed_mlp, grad_gate),
        row_product(normed_mlp, grad_upward),
        row_product(active, grad_down_in),
    )
    return (grad_input, terms)


def body(
    tokens, segments, cotangent, w_qkv, b_qkv, w_out, gain_attn, gain_mlp, w_gate, w_up, w_down
):
    is_first = lax.axis_index("section") == 0
    shards = (w_qkv, b_qkv, w_out, gain_attn, gain_mlp, w_gate, w_up, w_down)
    gathered = (
        lax.all_gather(shards[0], "fsdp", axis=1, tiled=True),
        lax.all_gather(shards[1], "fsdp", axis=1, tiled=True),
        *sent_together((shards[2], shards[3], shards[4], shards[5], shards[6]), "fsdp", 1, 2),
        lax.all_gather(shards[7], "fsdp", axis=1, tiled=True),
    )
    forward_params = tuple((item[0] for item in gathered))
    seg_blocks = segments.reshape(MB, ROWS)
    token_blocks = tokens.reshape(MB, ROWS, D)
    cot_blocks = cotangent.reshape(MB, ROWS, D)
    received = jnp.zeros((ROWS, D), jnp.bfloat16)
    inputs = []
    outputs = []
    for tick in range(MB + 1):
        own_block = min(tick, MB - 1)
        stream_in = jnp.where(is_first, token_blocks[own_block], received)
        segment = jnp.where(is_first, seg_blocks[own_block], seg_blocks[max(tick - 1, 0)])
        output, unused = layer_ahead(forward_params, stream_in, segment)
        inputs.append(stream_in)
        sent = output.astype(jnp.bfloat16)
        outputs.append(sent)
        if tick < MB:
            received = shifted(sent, "section", 1)
    states = jnp.stack(
        [jnp.where(is_first, outputs[batch], outputs[batch + 1]) for batch in range(MB)]
    )
    states = states.reshape(1, MB * ROWS, D)
    incoming = jnp.zeros((ROWS, D), jnp.bfloat16)
    grad_list = []
    sent_list = []
    totals = None
    for tick in range(MB + 1):
        first_batch = max(tick - 1, 0)
        last_batch = min(tick, MB - 1)
        valid = jnp.where(is_first, tick >= 1, tick < MB).astype(jnp.float32)
        grad_out = jnp.where(is_first, incoming, cot_blocks[last_batch]).astype(jnp.float32) * valid
        stream_in = jnp.where(is_first, inputs[first_batch], inputs[last_batch + 1])
        segment = jnp.where(is_first, seg_blocks[first_batch], seg_blocks[last_batch])
        unused, cache = layer_ahead(forward_params, stream_in, segment)
        grad_input, terms = layer_back(forward_params, cache, grad_out, segment)
        if totals is None:
            totals = terms
        else:
            totals = tuple((left + right for left, right in zip(totals, terms)))
        grad_sent = grad_input.astype(jnp.bfloat16)
        grad_list.append(grad_input)
        sent_list.append(grad_sent)
        if tick < MB:
            incoming = shifted(grad_sent, "section", -1)
    input_grads = jnp.stack(
        [
            jnp.where(is_first, grad_list[batch + 1], sent_list[batch].astype(jnp.float32))
            for batch in range(MB)
        ]
    ).reshape(1, MB * ROWS, D)
    stacked = tuple((item[None] for item in totals))
    shares = sum_packed(
        (
            stacked[0],
            stacked[1],
            stacked[2],
            stacked[3],
            stacked[4],
            stacked[5],
            stacked[6],
            stacked[7],
        ),
        "fsdp",
        (1, 1, 1, 1, 1, 1, 1, 1),
    )
    return (
        states,
        input_grads,
        shares[0],
        shares[1],
        shares[2],
        shares[3],
        shares[4],
        shares[5],
        shares[6],
        shares[7],
    )


def solution(mesh):
    return jax.shard_map(
        body,
        mesh=mesh,
        in_specs=(
            P("fsdp", None),
            P("fsdp"),
            P("fsdp", None),
            P("section", "fsdp", None),
            P("section", "fsdp"),
            P("section", "fsdp", None),
            P("section", "fsdp"),
            P("section", "fsdp"),
            P("section", "fsdp", None),
            P("section", "fsdp", None),
            P("section", "fsdp", None),
        ),
        out_specs=(
            P("section", "fsdp", None),
            P("section", "fsdp", None),
            P("section", "fsdp", None),
            P("section", "fsdp"),
            P("section", "fsdp", None),
            P("section", "fsdp"),
            P("section", "fsdp"),
            P("section", "fsdp", None),
            P("section", "fsdp", None),
            P("section", "fsdp", None),
        ),
        check_vma=False,
    )
```

profile of v0, /device:TPU:0, one launch (start us, length us, event | category | flops | bytes accessed | tf_op | source)
XLA Modules:
  0.0 1483.6 jit_solution(12185033863823215930)
XLA Ops:
  20.5 182.1 %all-reduce.1 = bf16[1152]{0:T(1024)(128)(2,1)S(1)} all-reduce(bf16[1152]{0:T(1024)(128)(2,1)S(1)} %dynamic-update-slice), channel_id=1, replica_groups=mesh['section'=2,'fsdp'=64] {'fsdp'}, use_global_device_ids=true, to_apply=%add.1 | all-reduce | flops 1152 | bytes 4608
  207.6 12.3 copy.406
  219.8 150.4 %all-gather.4.cloned.1.call-done = bf16[1,896,10626]{2,0,1:T(2,128)(2,1)} async-done(((bf16[1,14,10626]{2,0,1:T(2,128)(2,1)}), bf16[1,896,10626]{2,0,1:T(2,128)(2,1)}) %all-gather.4.cloned.1.call-update) | async-done | bytes 19041808 | tf_op jit(solution)/shard_map/all_gather | solution.py:25
  384.8 95.0 %fusion.305 = (bf16[1,896,4864]{2,0,1:T(2,128)(2,1)}, bf16[1,896,4864]{2,0,1:T(2,128)(2,1)}) fusion(bf16[1,896,10626]{2,0,1:T(2,128)(2,1)} %all-gather.4.cloned.1.call-done), kind=kLoop, calls=%fused_computation.473 | loop fusion | bytes 34865152 | tf_op jit(solution)/shard_map/split | solution.py:26
  479.8 19.5 %copy_bitcast_fusion = (bf16[896,4864]{1,0:T(8,128)(2,1)}, bf16[896,4864]{1,0:T(8,128)(2,1)S(1)}) fusion(bf16[1,896,4864]{2,0,1:T(2,128)(2,1)} %get-tuple-element.33, bf16[1,896,4864]{2,0,1:T(2,128)(2,1)} %get-tuple-element.32), kind=kLoop, calls=%fused_computation.6 | loop fusion | bytes 34865152 | tf_op jit(solution)/shard_map/squeeze | solution.py:261
  502.6 9.6 fusion.63
  532.9 9.6 fusion.60
  644.9 8.6 fusion.339
  692.9 8.5 fusion.338
  701.4 8.5 fusion.340
  787.3 19.3 %add_add_fusion.2 = f32[896,4864]{1,0:T(8,128)} fusion(f32[896,4864]{1,0:T(8,128)} %fusion.337, f32[896,4864]{1,0:T(8,128)} %fusion.338, bf16[64,896]{1,0:T(8,128)(2,1)S(1)} %copy-done.26, bf16[64,4864]{1,0:T(8,128)(2,1)S(1)} %copy-done.46), kind=kOutput, calls=%fused_computation.5 | convolution fusion | flops 566558720 | bytes 53035008 | tf_op jit(solution)/shard_map/dot_general | solution.py:97
  806.7 16.1 %reshape_transpose_reshape_broadcast_in_dim.20 = f32[64,68096]{1,0:T(8,128)} reshape(f32[896,4864]{1,0:T(8,128)} %add_add_fusion.2) | data formatting | bytes 34865152 | tf_op jit(solution)/shard_map/reshape;transpose;reshape;broadcast_in_dim | solution.py:47
  822.8 19.4 %add_add_fusion.1 = f32[896,4864]{1,0:T(8,128)} fusion(f32[896,4864]{1,0:T(8,128)} %fusion.339, f32[896,4864]{1,0:T(8,128)} %fusion.340, bf16[64,896]{1,0:T(8,128)(2,1)S(1)} %copy-done.26, bf16[64,4864]{1,0:T(8,128)(2,1)S(1)} %copy-done.44), kind=kOutput, calls=%fused_computation.4 | convolution fusion | flops 566558720 | bytes 53035008 | tf_op jit(solution)/shard_map/dot_general | solution.py:97
  842.2 16.2 %reshape_transpose_reshape_broadcast_in_dim.21 = f32[64,68096]{1,0:T(8,128)} reshape(f32[896,4864]{1,0:T(8,128)} %add_add_fusion.1) | data formatting | bytes 34865152 | tf_op jit(solution)/shard_map/reshape;transpose;reshape;broadcast_in_dim | solution.py:47
  858.4 18.8 %add_add_fusion = f32[4864,896]{1,0:T(8,128)} fusion(f32[4864,896]{1,0:T(8,128)} %fusion.81, f32[4864,896]{1,0:T(8,128)} %fusion.82, f32[64,4864]{1,0:T(8,128)S(1)} %copy-done.17, f32[64,4864]{1,0:T(8,128)S(1)} %copy-done.15, bf16[64,896]{1,0:T(8,128)(2,1)S(1)} %copy-done.88, f32[]{:T(128)S(6)} %convert_element_type.479), kind=kOutput, calls=%fused_computation.3 | convolution fusion | flops 568598528 | bytes 54902788 | tf_op jit(solution)/shard_map/dot_general | solution.py:97
  877.2 15.7 %reshape_transpose_reshape_broadcast_in_dim.22 = f32[64,68096]{1,0:T(8,128)} reshape(f32[4864,896]{1,0:T(8,128)} %add_add_fusion) | data formatting | bytes 34865152 | tf_op jit(solution)/shard_map/reshape;transpose;reshape;broadcast_in_dim | solution.py:47
  894.3 12.1 dynamic-update-slice.3
  909.6 50.8 %dynamic-update-slice.6 = f32[64,233006]{1,0:T(8,128)} dynamic-update-slice(f32[64,233006]{1,0:T(8,128)} %dynamic-update-slice.5, f32[64,68096]{1,0:T(8,128)} %reshape_transpose_reshape_broadcast_in_dim.20, s32[]{} %constant.80, s32[]{} %constant.85) | dynamic-update-slice | bytes 34865156
  960.4 50.8 %dynamic-update-slice.7 = f32[64,233006]{1,0:T(8,128)} dynamic-update-slice(f32[64,233006]{1,0:T(8,128)} %dynamic-update-slice.6, f32[64,68096]{1,0:T(8,128)} %reshape_transpose_reshape_broadcast_in_dim.21, s32[]{} %constant.80, s32[]{} %constant.86) | dynamic-update-slice | bytes 34865156
  1011.2 50.3 %dynamic-update-slice.8 = f32[64,233006]{1,0:T(8,128)} dynamic-update-slice(f32[64,233006]{1,0:T(8,128)} %dynamic-update-slice.7, f32[64,68096]{1,0:T(8,128)} %reshape_transpose_reshape_broadcast_in_dim.22, s32[]{} %constant.80, s32[]{} %constant.87) | dynamic-update-slice | bytes 34865156 | tf_op jit(solution)/shard_map/concatenate | solution.py:47
  1061.5 38.5 %pad.4 = f32[64,233472]{1,0:T(8,128)} pad(f32[64,233006]{1,0:T(8,128)} %dynamic-update-slice.8, f32[]{:T(128)} %constant.53.clone.1), padding=0_0x0_466 | pad | bytes 119418368 | tf_op jit(solution)/shard_map/jit(_pad)/pad | solution.py:49
  1100.0 57.9 %reshape.691 = f32[116736,128]{1,0:T(8,128)} reshape(f32[64,233472]{1,0:T(8,128)} %pad.4) | data formatting | bytes 119537664 | tf_op jit(solution)/shard_map/reshape | solution.py:49
  1166.7 9.7 fusion.78
  1178.1 288.8 %reduce-scatter.2.cloned.1.call-done = f32[1824,128]{1,0:T(8,128)} async-done(((f32[116736,128]{1,0:T(8,128)}), f32[1824,128]{1,0:T(8,128)}) %reduce-scatter.2.cloned.1.call-update) | async-done | bytes 933904 | tf_op jit(solution)/shard_map/reduce_scatter | solution.py:50
  (687 shorter events, 297.5 us)
Async XLA Ops:
  7.2 195.5 %copy-start.170 = (s32[128]{0:T(128)S(1)}, s32[128]{0:T(128)}, u32[]{:S(2)}) copy-start(s32[128]{0:T(128)} %param.12) | copy-start | bytes 1540
  7.2 195.8 %copy-start.40 = (bf16[128,896]{1,0:T(8,128)(2,1)S(1)}, bf16[128,896]{1,0:T(8,128)(2,1)}, u32[]{:S(2)}) copy-start(bf16[128,896]{1,0:T(8,128)(2,1)} %param.11) | copy-start | bytes 688132
  7.2 197.8 %all-gather.6.cloned.1.call-start = ((), (), s32[]{:S(2)}) async-start(), calls=%async_computation.2 | async-start | bytes 4193280 | tf_op jit(solution)/shard_map/all_gather | solution.py:256
  8.8 198.8 %all-gather.8.cloned.1.call-start = ((), (), s32[]{:S(2)}) async-start(), calls=%async_computation.3 | async-start | bytes 17704960 | tf_op jit(solution)/shard_map/all_gather | solution.py:259
  10.7 359.5 %all-gather.4.cloned.1.call-start = ((), (), s32[]{:S(2)}) async-start(), calls=%async_computation.1 | async-start | bytes 39137280 | tf_op jit(solution)/shard_map/all_gather | solution.py:25
  19.0 1448.0 %reduce-scatter.2.cloned.1.call-start = ((), (), s32[]{:S(2)}) async-start(), calls=%async_computation.4 | async-start | bytes 60702720 | tf_op jit(solution)/shard_map/reduce_scatter | solution.py:50
  204.0 178.3 %copy-start.142 = (pred[64,64]{0,1:T(8,128)(4,1)}, pred[64,64]{0,1:T(8,128)(4,1)S(1)}, u32[]{:S(2)}) copy-start(pred[64,64]{0,1:T(8,128)(4,1)S(1)} %get-tuple-element.164) | copy-start | bytes 12292
  205.0 176.8 %copy-start.72 = (f32[64,32]{1,0:T(8,128)}, f32[64,32]{1,0:T(8,128)S(1)}, u32[]{:S(2)}) copy-start(f32[64,32]{1,0:T(8,128)S(1)} %get-tuple-element.121) | copy-start | bytes 24580
  205.0 176.8 %copy-start.75 = (f32[64,32]{1,0:T(8,128)}, f32[64,32]{1,0:T(8,128)S(1)}, u32[]{:S(2)}) copy-start(f32[64,32]{1,0:T(8,128)S(1)} %get-tuple-element.122) | copy-start | bytes 24580
  377.0 369.2 %copy-start.54 = (f32[896]{0:T(1024)}, f32[896]{0:T(1024)S(1)}, u32[]{:S(2)}) copy-start(f32[896]{0:T(1024)S(1)} %get-tuple-element.10) | copy-start | bytes 10756
  377.0 387.5 %copy-start.85 = (f32[896]{0:T(1024)}, f32[896]{0:T(1024)S(1)}, u32[]{:S(2)}) copy-start(f32[896]{0:T(1024)S(1)} %get-tuple-element.11) | copy-start | bytes 10756
  384.8 114.5 %copy-start.166 = (f32[64]{0:T(128)}, f32[64]{0:T(128)S(1)}, u32[]{:S(2)}) copy-start(f32[64]{0:T(128)S(1)} %add_rsqrt_fusion.10) | copy-start | bytes 772
  512.2 3.2 collective-permute-start
  516.5 33.2 %copy-start.24 = (bf16[64,896]{1,0:T(8,128)(2,1)}, bf16[64,896]{1,0:T(8,128)(2,1)S(1)}, u32[]{:S(2)}) copy-start(bf16[64,896]{1,0:T(8,128)(2,1)S(1)} %get-tuple-element.30) | copy-start | bytes 344068
  542.6 8.9 collective-permute-start.1
  554.3 14.7 copy-start.19
  662.2 7.1 collective-permute-start.2
  670.2 13.7 slice-start.15
  670.2 13.7 slice-start.16
  726.8 6.8 collective-permute-start.3
  806.7 16.1 %copy-start.44 = (bf16[64,4864]{1,0:T(8,128)(2,1)S(1)}, bf16[64,4864]{1,0:T(8,128)(2,1)}, u32[]{:S(2)}) copy-start(bf16[64,4864]{1,0:T(8,128)(2,1)} %copy-done.43) | copy-start | bytes 1867780
  842.2 16.2 %copy-start.15 = (f32[64,4864]{1,0:T(8,128)S(1)}, f32[64,4864]{1,0:T(8,128)}, u32[]{:S(2)}) copy-start(f32[64,4864]{1,0:T(8,128)} %fusion.335) | copy-start | bytes 3735556
  842.2 16.2 %copy-start.17 = (f32[64,4864]{1,0:T(8,128)S(1)}, f32[64,4864]{1,0:T(8,128)}, u32[]{:S(2)}) copy-start(f32[64,4864]{1,0:T(8,128)} %fusion.334) | copy-start | bytes 3735556
  842.2 16.2 %copy-start.88 = (bf16[64,896]{1,0:T(8,128)(2,1)S(1)}, bf16[64,896]{1,0:T(8,128)(2,1)}, u32[]{:S(2)}) copy-start(bf16[64,896]{1,0:T(8,128)(2,1)} %copy-done.87) | copy-start | bytes 344068
  (185 other events, 851.9 us)
Sparse Core Ops, SparseCore 0:
  11.5 71.3 all-gather.5
  86.3 104.3 all-gather.7
  193.5 176.6 all-gather.3
  1158.0 308.8 reduce-scatter.1
where the time goes:
time: 1490 us; the launch traced here: 1480 us
  local copies, waits for them, and re-layouts  527 us (35%)
  waiting for transfers between devices  439 us (29%)
  matrix products  274 us (18%)
  blocking collectives  182 us (12%)
  other arithmetic  35.8 us (2%)
  between operations  17.7 us (1%)
    reduce_scatter x1, waiting for transfers between devices, sum_packed(): lax.psum_scatter(lines, axis, tiled=True).reshape(-1)  289 us
    unnamed x1, blocking collectives  182 us
    unnamed x416, local copies, waits for them, and re-layouts  164 us
    all_gather x1, waiting for transfers between devices, sent_together(): filled = lax.all_gather(both, axis, axis=dim, tiled=True)  150 us
    dot_general x15, matrix products, row_product(): lax.dot_general(left, right, (((0,), (0,)), ((), ())), preferred_element_...  127 us
    split x3, local copies, waits for them, and re-layouts, sent_together(): jnp.split(filled, [sum(widths[:k]) for k in range(1, len(widths))], axis=...  96.9 us
    reshape x1, local copies, waits for them, and re-layouts, sum_packed(): jnp.pad(lines, ((0, 0), (0, span * 128 - lines.shape[1]))).reshape(-1, 128)  57.9 us
    another operation x5, local copies, waits for them, and re-layouts, sum_packed(): lines = jnp.concatenate([b.reshape(devices, -1) for b in pieces], axis=1)  57.8 us
  transfers between devices with their start and end apart: 8, of which 2 were waited for; matrix products, arithmetic and copies ran while one was open for 4% of the time, Pallas kernels for 0%

commit v1 on v0

v1 whole, which is shorter than its diff:
```python
import functools

import jax
import jax.numpy as jnp
import numpy as np
from jax import lax
from jax.experimental import pallas as pl
from jax.experimental.pallas import tpu as pltpu
from jax.sharding import PartitionSpec as P

D = 896
QH = 14
KVH = 2
HD = 64
FF = 4864
QKV = 1152
ROWS = 64
TOK = 128
RING = 4

DP = 1024
FP = 1280
ATT = QKV + DP
N_SEM = 96

eps_norm = 1e-06
theta_base = 1000000.0
MESH = pl.DeviceIdType.MESH
F32 = jnp.float32
BF16 = jnp.bfloat16


def dot(left, right):
    return jnp.dot(left, right, preferred_element_type=F32)


def dot_back(left, right):
    return lax.dot_general(left, right, (((1,), (1,)), ((), ())), preferred_element_type=F32)


def dot_rows(left, right):
    return lax.dot_general(left, right, (((0,), (0,)), ((), ())), preferred_element_type=F32)


def times(n, step):
    def run(i, carry):
        step(i)
        return carry

    lax.fori_loop(0, n, run, 0)


def span(start, size, unit):
    return pl.ds(pl.multiple_of(start, unit), size)


def kernel(
    tok, cot, cos_t, sin_t, mask, gu_in, d_in, qkv_in, out_in, pad_s,
    states, igrads, ogu, od, oqkv, oout,
    w_att, w_gu, w_d, g_att,
    xin, dyin, ybuf, dxbuf, h1, obuf, do_buf, datt, dp_buf,
    h2all, dmall, gact, aact, dgu, h2t, at,
    part_f, part_b, af1, af2, ab1, ab2, dh,
    u1, u2, x1, proj, qs, kd, vd, probs,
    zg1, zg2, xg1, xg2, yg, xd1, xd2, zd1, zd2, ya1, ya2, xa1, xa2, za1, za2,
    send, recv,
):
    sec = lax.axis_index("section")
    me = lax.axis_index("fsdp")
    z, x, y = me // 16, lax.rem(me // 4, 4), lax.rem(me, 4)
    up1 = lambda c: lax.rem(c + 1, RING)
    up2 = lambda c: lax.rem(c + 2, RING)
    up3 = lambda c: lax.rem(c + 3, RING)

    def at_z(c):
        return (sec, c * 16 + x * 4 + y)

    def at_x(c):
        return (sec, z * 16 + c * 4 + y)

    def at_y(c):
        return (sec, z * 16 + x * 4 + c)

    other = (1 - sec, me)
    barrier = pltpu.get_barrier_semaphore()
    partners = [
        at_z(up1(z)), at_z(up3(z)), at_x(up1(x)), at_x(up3(x)),
        at_y(up1(y)), at_y(up3(y)), at_y(up2(y)), other,
    ]
    for dev in partners:
        pl.semaphore_signal(barrier, inc=1, device_id=dev, device_id_type=MESH)

    count = [0]
    pending = []

    def remote(src, dst, dev):
        k = count[0]
        count[0] += 1
        cp = pltpu.make_async_remote_copy(
            src_ref=src, dst_ref=dst, send_sem=send.at[k], recv_sem=recv.at[k],
            device_id=dev, device_id_type=MESH,
        )
        return cp

    def go(src, dst, dev):
        cp = remote(src, dst, dev)
        cp.start()
        pending.append(cp)
        return cp

    class Gather:
        def __init__(self, blk, low, high, c, dev):
            self.blk, self.low, self.high, self.c, self.dev = blk, low, high, c, dev

        def start(self):
            c = self.c
            self.a = go(self.blk(c), self.blk(c), self.dev(up1(c)))
            self.b = go(self.blk(c), self.blk(c), self.dev(up3(c)))

        def mid(self):
            c = self.c
            self.a.wait_recv()
            self.e = go(self.low(up3(c)), self.low(up3(c)), self.dev(up1(c)))
            self.b.wait_recv()
            self.f = go(self.high(up1(c)), self.high(up1(c)), self.dev(up3(c)))

        def end(self):
            self.e.wait_recv()
            self.f.wait_recv()

    class Reduce:
        def __init__(self, blk, low, high, c, dev, r1, r2, add):
            self.blk, self.low, self.high, self.c, self.dev = blk, low, high, c, dev
            self.r1, self.r2, self.add = r1, r2, add

        def start(self):
            c = self.c
            self.a = go(self.low(up2(c)), self.r1.at[0], self.dev(up1(c)))
            self.b = go(self.high(up2(c)), self.r1.at[1], self.dev(up3(c)))

        def mid(self):
            c = self.c
            self.a.wait_recv()
            self.add(up1(c), 0, self.r1.at[0])
            self.e = go(self.blk(up1(c)), self.r2.at[0], self.dev(up1(c)))
            self.b.wait_recv()
            self.add(up3(c), 1, self.r1.at[1])
            self.f = go(self.blk(up3(c)), self.r2.at[1], self.dev(up3(c)))

        def end(self):
            self.e.wait_recv()
            self.f.wait_recv()

    mine_d = span(320 * x + 80 * z, 80, 16)
    mine_gu = span(256 * z + 64 * x + 16 * y, 16, 16)
    w_d[mine_d, :] = dot(d_in[...], pad_s[...]).astype(BF16)
    w_gu[mine_gu, :] = gu_in[y]
    w_att[z, x, y, :, :QKV] = qkv_in[...]
    w_att[z, x, y, :, QKV:] = dot(out_in[...], pad_s[...]).astype(BF16)
    pl.semaphore_wait(barrier, len(partners))

    gu_copies = []
    for step in (up1, up3, up2):
        gu_copies.append(go(gu_in.at[step(y)], w_gu.at[mine_gu], at_y(step(y))))
    att_z = Gather(
        lambda c: w_att.at[c, x, y],
        lambda c: w_att.at[c, x, y, :, pl.ds(0, QKV)],
        lambda c: w_att.at[c, x, y, :, pl.ds(QKV, DP)], z, at_z)
    att_x = Gather(
        lambda c: w_att.at[:, c, y],
        lambda c: w_att.at[:, c, y, :, pl.ds(0, QKV)],
        lambda c: w_att.at[:, c, y, :, pl.ds(QKV, DP)], x, at_x)
    att_y = Gather(
        lambda c: w_att.at[:, :, c],
        lambda c: w_att.at[:, :, c, :, pl.ds(0, QKV)],
        lambda c: w_att.at[:, :, c, :, pl.ds(QKV, DP)], y, at_y)
    gu_x = Gather(
        lambda c: w_gu.at[span(256 * z + 64 * c, 64, 64)],
        lambda c: w_gu.at[span(256 * z + 64 * c, 64, 64), pl.ds(0, FP)],
        lambda c: w_gu.at[span(256 * z + 64 * c, 64, 64), pl.ds(FP, FP)], x, at_x)
    gu_z = Gather(
        lambda c: w_gu.at[span(256 * c, 256, 256)],
        lambda c: w_gu.at[span(256 * c, 256, 256), pl.ds(0, FP)],
        lambda c: w_gu.at[span(256 * c, 256, 256), pl.ds(FP, FP)], z, at_z)
    d_z = Gather(
        lambda c: w_d.at[span(320 * x + 80 * c, 80, 16)],
        lambda c: w_d.at[span(320 * x + 80 * c, 80, 16), pl.ds(0, 512)],
        lambda c: w_d.at[span(320 * x + 80 * c, 80, 16), pl.ds(512, 512)], z, at_z)
    d_x = Gather(
        lambda c: w_d.at[span(320 * c, 320, 64)],
        lambda c: w_d.at[span(320 * c, 320, 64), pl.ds(0, 512)],
        lambda c: w_d.at[span(320 * c, 320, 64), pl.ds(512, 512)], x, at_x)
    att_z.start()
    d_z.start()
    for cp in gu_copies:
        cp.wait_recv()
    gu_x.start()
    att_z.mid()
    d_z.mid()
    gu_x.mid()
    att_z.end()
    att_x.start()
    gu_x.end()
    gu_z.start()
    d_z.end()
    d_x.start()
    att_x.mid()
    att_x.end()
    att_y.start()
    d_x.mid()
    att_y.mid()
    att_y.end()

    send_y = remote(ybuf, xin, other)
    send_dx = remote(dxbuf, dyin, other)

    @pl.when(sec == 0)
    def _():
        xin[...] = dot(tok[...], pad_s[...]).astype(BF16)

    @pl.when(sec == 1)
    def _():
        dyin[...] = dot(cot[...], pad_s[...]).astype(BF16)

    gu_z.mid()
    d_x.end()
    gu_z.end()

    @pl.when(sec == 1)
    def _():
        send_y.wait_recv()

    lanes = lax.broadcasted_iota(jnp.int32, (TOK, DP), 1)
    slot = lax.rem(lanes, 16)
    picks = lax.broadcasted_iota(jnp.int32, (8, DP), 1)
    pick15 = jnp.where(lax.rem(picks, 16) == 15, 1.0, 0.0).astype(BF16)
    pick14 = jnp.where(lax.rem(picks, 16) == 14, 1.0, 0.0).astype(BF16)
    lane = lax.broadcasted_iota(jnp.int32, (TOK, 128), 1)
    low_half = lane < HD
    first = lax.rem(lane, HD) < HD // 2

    def att_weight(start, size):
        return w_att[:, :, :, :, pl.ds(start, size)].reshape(DP, size)

    def swap(tile):
        return jnp.where(first, pltpu.roll(tile, 96, 1), pltpu.roll(tile, 32, 1))

    def gain_rows():
        ga = dot(pick15, att_weight(0, D)).astype(BF16)
        ga = dot(ga, pad_s[...])
        gm = dot(pick14, att_weight(QKV, DP))
        return ga[0:1], gm[0:1]

    def stack(tile_of, kv, ref):
        for j in range(7):
            head = kv * 7 + j
            keep = low_half if head % 2 == 0 else ~low_half
            ref[kv, pl.ds(j * 128, 128), :] = jnp.where(keep, tile_of(head // 2), 0.0).astype(BF16)

    stream = xin[...].astype(F32)
    inv1 = lax.rsqrt(jnp.sum(stream * stream, axis=1, keepdims=True) * (1.0 / D) + eps_norm)
    gain_a, gain_m = gain_rows()
    unit1 = stream * inv1
    u1[...] = unit1
    h1[...] = jnp.where(slot == 14, 1.0, unit1 * gain_a).astype(BF16)

    def project(i):
        cols = span(i * 384, 384, 128)
        proj[:, cols] = dot(h1[...], w_att[:, :, :, :, cols].reshape(DP, 384))

    times(3, project)

    def rotated(j):
        tile = proj[:, pl.ds(128 * j, 128)]
        return tile * cos_t[...] + swap(tile) * sin_t[...]

    def both(tile):
        rolled = pltpu.roll(tile, HD, 1)
        return (
            jnp.where(low_half, tile, rolled).astype(BF16),
            jnp.where(low_half, rolled, tile).astype(BF16),
        )

    for kv in range(KVH):
        stack(rotated, kv, qs)
    kd[0], kd[1] = both(rotated(7))
    vd[0], vd[1] = both(proj[:, pl.ds(1024, 128)])
    allowed = mask[...] > 0.5

    for kv in range(KVH):

        def attend(j, kv=kv):
            rows = span(j * 128, 128, 128)
            s = dot_back(qs[kv, rows, :], kd[kv]) * HD ** (-0.5)
            s = jnp.where(allowed, s, -1e30)
            weights = jnp.exp(s - jnp.max(s, axis=1, keepdims=True))
            probs[kv, rows, :] = weights / jnp.sum(weights, axis=1, keepdims=True)

        times(7, attend)

    def head_out(head):
        kv, j = divmod(head, 7)
        return dot(probs[kv, pl.ds(j * 128, 128), :].astype(BF16), vd[kv])

    mixed = [jnp.where(low_half, head_out(2 * t), head_out(2 * t + 1)).astype(BF16) for t in range(7)]
    obuf[...] = dot(jnp.concatenate(mixed, axis=1), pad_s[...]).astype(BF16)

    def out_project(i):
        cols = span(i * 256, 256, 256)
        x1[:, cols] = xin[:, cols].astype(F32) + dot(
            obuf[...], w_att[:, :, :, :, span(QKV + i * 256, 256, 128)].reshape(DP, 256))

    times(4, out_project)
    middle = x1[...]
    inv2 = lax.rsqrt(jnp.sum(middle * middle, axis=1, keepdims=True) * (1.0 / D) + eps_norm)
    unit2 = middle * inv2
    u2[...] = unit2
    h2all[y] = (unit2 * gain_m).astype(BF16)

    def act_add(part, r):
        def add(c, half, got):
            cols = pl.ds(512 * half, 512)
            part[c, :, cols] = (part[c, :, cols].astype(F32) + got[...].astype(F32)).astype(BF16)

        return add

    def act_gather(ref):
        return Gather(
            lambda c: ref.at[c],
            lambda c: ref.at[c, :, pl.ds(0, 512)],
            lambda c: ref.at[c, :, pl.ds(512, 512)], y, at_y)

    def act_reduce(part, r1, r2):
        return Reduce(
            lambda c: part.at[c],
            lambda c: part.at[c, :, pl.ds(0, 512)],
            lambda c: part.at[c, :, pl.ds(512, 512)], y, at_y, r1, r2, act_add(part, r1))

    def mlp_chunk(c):
        def hidden(i):
            cols = span(i * 256, 256, 256)
            cols_up = span(FP + i * 256, 256, 256)
            gate = dot(h2all[c], w_gu[:, cols])
            upward = dot(h2all[c], w_gu[:, cols_up])
            gact[c, :, cols] = gate
            gact[c, :, cols_up] = upward
            aact[c, :, cols] = (gate * jax.nn.sigmoid(gate) * upward).astype(BF16)

        times(5, hidden)

        def down(i):
            cols = span(i * 256, 256, 256)
            part_f[c, :, cols] = dot(aact[c], w_d[:, cols]).astype(BF16)

        times(4, down)

    ag = act_gather(h2all)
    ag.start()
    mlp_chunk(y)
    ag.mid()
    mlp_chunk(up1(y))
    mlp_chunk(up3(y))
    ag.end()
    mlp_chunk(up2(y))
    rs = act_reduce(part_f, af1, af2)
    rs.start()
    rs.mid()
    rs.end()
    out = x1[...] + (part_f[y].astype(F32) + af2[0].astype(F32) + af2[1].astype(F32))
    ybuf[...] = out.astype(BF16)

    @pl.when(sec == 0)
    def _():
        send_y.start()

    states[...] = dot_back(ybuf[...], pad_s[...]).astype(BF16)

    @pl.when(sec == 0)
    def _():
        send_dx.wait_recv()

    dmall[y] = dyin[...]

    def back_chunk(c):
        def hidden(i):
            cols = span(i * 256, 256, 256)
            cols_up = span(FP + i * 256, 256, 256)
            da = dot_back(dmall[c], w_d[cols, :])
            gate = gact[c, :, cols]
            sig = jax.nn.sigmoid(gate)
            dgu[c, :, cols] = (
                da * gact[c, :, cols_up] * (sig * (1.0 + gate * (1.0 - sig)))).astype(BF16)
            dgu[c, :, cols_up] = (da * gate * sig).astype(BF16)

        times(5, hidden)

        def back(i):
            cols = span(i * 256, 256, 256)
            part_b[c, :, cols] = dot_back(dgu[c], w_gu[cols, :]).astype(BF16)

        times(4, back)

    ag = act_gather(dmall)
    ag.start()
    back_chunk(y)
    ag.mid()
    back_chunk(up1(y))
    back_chunk(up3(y))
    ag.end()
    back_chunk(up2(y))
    rs = act_reduce(part_b, ab1, ab2)
    rs.start()

    g_gu, g_d = w_gu, w_d
    for cp in pending:
        cp.wait_send()
    pending.clear()
    for c in range(RING):
        cols = pl.ds(128 * c, 128)
        h2t[:, cols] = h2all[c].T
        at[:, cols] = aact[c].T
    rs.mid()

    def grad_gu(i):
        cols = span(lax.rem(i, 10) * 256, 256, 256)
        rows = span((i // 10) * 256, 256, 256)
        g_gu[rows, cols] = dot(h2t[rows, :], dgu[:, :, cols].reshape(512, 256)).astype(BF16)

    times(40, grad_gu)

    gu_rows = lambda c: span(256 * c, 256, 256)
    gu_rows_x = lambda c: span(256 * z + 64 * c, 64, 64)
    d_rows_x = lambda c: span(320 * c, 320, 64)
    d_rows_z = lambda c: span(320 * x + 80 * c, 80, 16)

    def flat_add(ref, rows_of, n, width, unit):
        def add(c, half, got):
            cols = pl.ds(width * half, width)
            base = rows_of(c).start

            def step(i):
                there = span(base + unit * i, unit, 16)
                here = span(unit * i, unit, 16)
                ref[there, cols] = (
                    ref[there, cols].astype(F32) + got[here, :].astype(F32)).astype(BF16)

            times(n // unit, step)

        return add

    def flat_total(ref, rows_of, c, n, r2, unit):
        base = rows_of(c).start

        def step(i):
            there = span(base + unit * i, unit, 16)
            here = span(unit * i, unit, 16)
            ref[there, :] = (
                ref[there, :].astype(F32) + r2[0, here, :].astype(F32) + r2[1, here, :].astype(F32)
            ).astype(BF16)

        times(n // unit, step)

    def flat_reduce(ref, rows_of, n, width, c, dev, r1, r2, unit):
        return Reduce(
            lambda k: ref.at[rows_of(k)],
            lambda k: ref.at[rows_of(k), pl.ds(0, width)],
            lambda k: ref.at[rows_of(k), pl.ds(width, width)],
            c, dev, r1, r2, flat_add(ref, rows_of, n, width, unit))

    rgu_z = flat_reduce(g_gu, gu_rows, 256, FP, z, at_z, zg1, zg2, 32)
    rgu_x = flat_reduce(g_gu, gu_rows_x, 64, FP, x, at_x, xg1, xg2, 32)
    rd_x = flat_reduce(g_d, d_rows_x, 320, 512, x, at_x, xd1, xd2, 64)
    rd_z = flat_reduce(g_d, d_rows_z, 80, 512, z, at_z, zd1, zd2, 16)
    rgu_z.start()

    def grad_d(i):
        cols = span(lax.rem(i, 4) * 256, 256, 256)
        rows = span((i // 4) * 256, 256, 256)
        g_d[rows, cols] = dot(at[rows, :], dmall[:, :, cols].reshape(512, 256)).astype(BF16)

    times(20, grad_d)
    rd_x.start()

    rs.end()
    dh2 = part_b[y].astype(F32) + ab2[0].astype(F32) + ab2[1].astype(F32)
    unit2 = u2[...]
    dgain_m = jnp.sum(dh2 * unit2, axis=0, keepdims=True)
    gu2 = dh2 * gain_m
    dx1 = dyin[...].astype(F32) + inv2 * (
        gu2 - unit2 * (jnp.sum(gu2 * unit2, axis=1, keepdims=True) * (1.0 / D)))
    x1[...] = dx1
    datt[...] = dx1.astype(BF16)

    def back_out(i):
        w = w_att[i, :, :, :, pl.ds(QKV, DP)].reshape(256, DP)
        do_buf[:, span(i * 256, 256, 256)] = dot_back(datt[...], w).astype(BF16)

    times(4, back_out)
    rgu_z.mid()
    do_c = dot_back(do_buf[...], pad_s[...])
    do_tile = lambda j: do_c[:, 128 * j : 128 * (j + 1)]
    dq_heads = [None] * QH
    dk_sum = []
    dv_sum = []
    for kv in range(KVH):
        dk = jnp.zeros((TOK, 128), F32)
        dv = jnp.zeros((TOK, 128), F32)
        for j in range(7):
            head = kv * 7 + j
            keep = low_half if head % 2 == 0 else ~low_half
            do_h = jnp.where(keep, do_tile(head // 2), 0.0).astype(BF16)
            pr = probs[kv, pl.ds(j * 128, 128), :]
            dpr = dot_back(do_h, vd[kv])
            ds = (pr * (dpr - jnp.sum(dpr * pr, axis=1, keepdims=True))).astype(BF16)
            dv = dv + dot_rows(pr.astype(BF16), do_h)
            dk = dk + dot_rows(ds, qs[kv, pl.ds(j * 128, 128), :])
            dq_heads[head] = dot(ds, kd[kv]) * HD ** (-0.5)
        dk_sum.append((dk + pltpu.roll(dk, HD, 1)) * HD ** (-0.5))
        dv_sum.append(dv + pltpu.roll(dv, HD, 1))

    def unrotated(tile):
        return (tile * cos_t[...] - swap(tile) * sin_t[...]).astype(BF16)

    for j in range(7):
        dp_buf[:, pl.ds(128 * j, 128)] = unrotated(
            jnp.where(low_half, dq_heads[2 * j], dq_heads[2 * j + 1]))
    dp_buf[:, pl.ds(896, 128)] = unrotated(jnp.where(low_half, dk_sum[0], dk_sum[1]))
    dp_buf[:, pl.ds(1024, 128)] = jnp.where(low_half, dv_sum[0], dv_sum[1]).astype(BF16)

    def back_proj(i):
        w = w_att[i, :, :, :, pl.ds(0, QKV)].reshape(256, QKV)
        dh[:, span(i * 256, 256, 256)] = dot_back(dp_buf[...], w)

    times(4, back_proj)
    dh1 = jnp.where(slot < 14, dh[...], 0.0)
    unit1 = u1[...]
    dgain_a = jnp.sum(dh1 * unit1, axis=0, keepdims=True)
    gu1 = dh1 * gain_a
    dx = x1[...] + inv1 * (
        gu1 - unit1 * (jnp.sum(gu1 * unit1, axis=1, keepdims=True) * (1.0 / D)))
    dx_hi = dx.astype(BF16)
    dxbuf[...] = dx_hi

    @pl.when(sec == 1)
    def _():
        send_dx.start()
        igrads[...] = dot_back(dx_hi, pad_s[...])

    @pl.when(sec == 0)
    def _():
        dx_lo = (dx - dx_hi.astype(F32)).astype(BF16)
        igrads[...] = dot_back(dx_hi, pad_s[...]) + dot_back(dx_lo, pad_s[...])

    h1t = h1[...].T
    ot = obuf[...].T
    proj[0:1, 0:DP] = dgain_a
    dh[0:1, :] = dgain_m
    h2t[:, 0:128] = h1t
    h2t[:, 128:256] = ot
    row = lax.rem(lax.broadcasted_iota(jnp.int32, (256, 256), 0), 16)
    row15 = row == 15
    row14 = row == 14

    def grad_qkv(i):
        zz, n = i // 4, lax.rem(i, 4)
        cols = span(n * 256, 256, 256)
        g = dot(h2t[span(zz * 256, 256, 256), 0:128], dp_buf[:, cols])
        g = jnp.where(row15, proj[0:1, cols], g)
        g_att[zz, :, :, :, cols] = g.astype(BF16).reshape(4, 4, 16, 256)
        g = dot(h2t[span(zz * 256, 256, 256), 128:256], datt[:, cols])
        g = jnp.where(row14, dh[0:1, cols], g)
        g_att[zz, :, :, :, span(QKV + n * 256, 256, 128)] = g.astype(BF16).reshape(4, 4, 16, 256)

    times(16, grad_qkv)

    def grad_v(zz):
        g = dot(h2t[span(zz * 256, 256, 256), 0:128], dp_buf[:, pl.ds(1024, 128)])
        g_att[zz, :, :, :, pl.ds(1024, 128)] = g.astype(BF16).reshape(4, 4, 16, 128)

    times(4, grad_v)

    half_cols = (pl.ds(0, QKV), pl.ds(QKV, DP))

    def add_y(c, half, got):
        cols = half_cols[half]
        size = cols.size

        def step(i):
            a, b = i // 4, lax.rem(i, 4)
            g_att[a, b, c, :, cols] = (
                g_att[a, b, c, :, cols].astype(F32) + got[a, b, :, pl.ds(0, size)].astype(F32)
            ).astype(BF16)

        times(16, step)

    def add_x(c, half, got):
        cols = half_cols[half]
        size = cols.size

        def step(a):
            g_att[a, c, y, :, cols] = (
                g_att[a, c, y, :, cols].astype(F32) + got[a, :, pl.ds(0, size)].astype(F32)
            ).astype(BF16)

        times(4, step)

    def add_z(c, half, got):
        cols = half_cols[half]
        size = cols.size
        g_att[c, x, y, :, cols] = (
            g_att[c, x, y, :, cols].astype(F32) + got[:, pl.ds(0, size)].astype(F32)
        ).astype(BF16)

    class AttReduce(Reduce):
        def start(self):
            c = self.c
            lead = (slice(None),) * self.lead
            low = self.r1.at[(0,) + lead]
            high = self.r1.at[(1,) + lead + (pl.ds(0, DP),)]
            self.a = go(self.low(up2(c)), low, self.dev(up1(c)))
            self.b = go(self.high(up2(c)), high, self.dev(up3(c)))

    def att_reduce(lead, blk, c, dev, r1, r2, add):
        red = AttReduce(
            lambda k: g_att.at[blk(k)],
            lambda k: g_att.at[blk(k) + (slice(None), half_cols[0])],
            lambda k: g_att.at[blk(k) + (slice(None), half_cols[1])],
            c, dev, r1, r2, add)
        red.lead = lead
        return red

    ra_y = att_reduce(3, lambda k: (slice(None), slice(None), k), y, at_y, ya1, ya2, add_y)
    ra_x = att_reduce(2, lambda k: (slice(None), k, y), x, at_x, xa1, xa2, add_x)
    ra_z = att_reduce(1, lambda k: (k, x, y), z, at_z, za1, za2, add_z)
    ra_y.start()
    rd_x.mid()
    ra_y.mid()
    rd_x.end()
    flat_total(g_d, d_rows_x, x, 320, xd2, 64)
    rd_z.start()
    rgu_z.end()
    flat_total(g_gu, gu_rows, z, 256, zg2, 16)
    rgu_x.start()
    ra_y.end()

    def total_y(i):
        a, b = i // 4, lax.rem(i, 4)
        g_att[a, b, y] = (
            g_att[a, b, y].astype(F32) + ya2[0, a, b].astype(F32) + ya2[1, a, b].astype(F32)
        ).astype(BF16)

    times(16, total_y)
    ra_x.start()
    rd_z.mid()
    rgu_x.mid()
    ra_x.mid()
    rd_z.end()
    here = d_rows_z(z)
    tot = g_d[here, :].astype(F32) + zd2[0].astype(F32) + zd2[1].astype(F32)
    hi = tot.astype(BF16)
    lo = (tot - hi.astype(F32)).astype(BF16)
    od[...] = dot_back(hi, pad_s[...]) + dot_back(lo, pad_s[...])
    rgu_x.end()
    flat_total(g_gu, gu_rows_x, x, 64, xg2, 16)
    last = []
    block = lambda c: span(256 * z + 64 * x + 16 * c, 16, 16)
    for step in (up1, up3, up2):
        last.append(go(g_gu.at[block(step(y))], yg.at[y], at_y(step(y))))
    ra_x.end()

    def total_x(a):
        g_att[a, x, y] = (
            g_att[a, x, y].astype(F32) + xa2[0, a].astype(F32) + xa2[1, a].astype(F32)
        ).astype(BF16)

    times(4, total_x)
    ra_z.start()
    ra_z.mid()
    ogu[y] = g_gu[block(y), :]
    for cp in last:
        cp.wait_recv()
    for step in (up1, up3, up2):
        ogu[step(y)] = yg[step(y)]
    ra_z.end()
    tot = g_att[z, x, y].astype(F32) + za2[0].astype(F32) + za2[1].astype(F32)
    oqkv[...] = tot[:, :QKV]
    tot = tot[:, QKV:]
    hi = tot.astype(BF16)
    lo = (tot - hi.astype(F32)).astype(BF16)
    oout[...] = dot_back(hi, pad_s[...]) + dot_back(lo, pad_s[...])

    for cp in pending:
        cp.wait_send()

    @pl.when(sec == 0)
    def _():
        send_y.wait_send()

    @pl.when(sec == 1)
    def _():
        send_dx.wait_send()


def pad_matrix():
    column = np.arange(DP)
    row = np.where(column % 16 < 14, 14 * (column // 16) + column % 16, -1)
    return (np.arange(D)[:, None] == row[None, :]).astype(jnp.bfloat16)


def tables(segments):
    seg = segments.reshape(TOK // ROWS, ROWS)
    earlier = jnp.sum((seg[:, None, :] < seg[:, :, None]).astype(jnp.int32), axis=2)
    place = (jnp.arange(ROWS, dtype=jnp.int32)[None] - earlier).astype(F32).reshape(TOK)
    half = HD // 2
    inverse = theta_base ** (-(jnp.arange(half, dtype=F32) * 2.0 / HD))
    angles = place[:, None] * jnp.tile(inverse, 4)[None, :]
    sign = jnp.where(jnp.arange(128) % HD < half, -1.0, 1.0).astype(F32)
    index = jnp.arange(TOK)
    allowed = (
        (segments[:, None] == segments[None, :])
        & (index[None, :] <= index[:, None])
        & (index[None, :] // ROWS == index[:, None] // ROWS)
    )
    return jnp.cos(angles), jnp.sin(angles) * sign, allowed.astype(F32)


def by_rank(weight):
    pieces = weight.reshape(14, 4, 4, 4, 76).transpose(3, 0, 2, 1, 4)
    return jnp.pad(pieces, ((0, 0), (0, 2), (0, 0), (0, 0), (0, 4))).reshape(4, 16, FP)


def from_rank(grad):
    pieces = grad.reshape(4, 16, 4, 4, 80)[:, :14, :, :, :76]
    return pieces.transpose(1, 3, 2, 0, 4).reshape(1, 14, FF).astype(F32)


def own_row(values, width):
    me = lax.axis_index("fsdp")
    lane = jnp.arange(width)
    n = values.shape[0]
    return jnp.where(lane // n == me, jnp.tile(values, width // n), 0).astype(BF16)[None]


def body(
    tokens, segments, cotangent, w_qkv, b_qkv, w_out, gain_attn, gain_mlp, w_gate, w_up, w_down
):
    me = lax.axis_index("fsdp")
    cos_t, sin_t, mask = tables(segments)
    gu_in = jnp.concatenate([by_rank(w_gate[0]), by_rank(w_up[0])], axis=2)
    d_in = jnp.pad(w_down[0], ((0, 4), (0, 0)))
    gain_row = jnp.pad(own_row(gain_attn[0], D), ((0, 0), (0, QKV - D)))
    qkv_in = jnp.concatenate([w_qkv[0], own_row(b_qkv[0], QKV), gain_row], axis=0)
    out_in = jnp.concatenate([w_out[0], own_row(gain_mlp[0], D), jnp.zeros((1, D), BF16)], axis=0)
    sds = jax.ShapeDtypeStruct
    vm = pltpu.VMEM
    states, igrads, ogu, od, oqkv, oout = pl.pallas_call(
        kernel,
        out_shape=(
            sds((TOK, D), BF16), sds((TOK, D), F32), sds((4, 16, 2 * FP), BF16),
            sds((80, D), F32), sds((16, QKV), F32), sds((16, D), F32),
        ),
        in_specs=[pl.BlockSpec(memory_space=pltpu.VMEM)] * 10,
        out_specs=tuple([pl.BlockSpec(memory_space=pltpu.VMEM)] * 6),
        scratch_shapes=[
            vm((4, 4, 4, 16, ATT), BF16), vm((DP, 2 * FP), BF16), vm((FP, DP), BF16),
            vm((4, 4, 4, 16, ATT), BF16),
            *[vm((TOK, DP), BF16)] * 8, vm((TOK, QKV), BF16),
            vm((4, TOK, DP), BF16), vm((4, TOK, DP), BF16), vm((4, TOK, 2 * FP), F32),
            vm((4, TOK, FP), BF16), vm((4, TOK, 2 * FP), BF16), vm((DP, 512), BF16), vm((FP, 512), BF16),
            vm((4, TOK, DP), BF16), vm((4, TOK, DP), BF16),
            vm((2, TOK, 512), BF16), vm((2, TOK, DP), BF16),
            vm((2, TOK, 512), BF16), vm((2, TOK, DP), BF16), vm((TOK, DP), F32),
            vm((TOK, DP), F32), vm((TOK, DP), F32), vm((TOK, DP), F32), vm((TOK, QKV), F32),
            vm((2, 7 * TOK, 128), BF16), vm((2, TOK, 128), BF16), vm((2, TOK, 128), BF16),
            vm((2, 7 * TOK, 128), F32),
            vm((2, 256, FP), BF16), vm((2, 256, 2 * FP), BF16),
            vm((2, 64, FP), BF16), vm((2, 64, 2 * FP), BF16), vm((4, 16, 2 * FP), BF16),
            vm((2, 320, 512), BF16), vm((2, 320, DP), BF16),
            vm((2, 80, 512), BF16), vm((2, 80, DP), BF16),
            vm((2, 4, 4, 16, QKV), BF16), vm((2, 4, 4, 16, ATT), BF16),
            vm((2, 4, 16, QKV), BF16), vm((2, 4, 16, ATT), BF16),
            vm((2, 16, QKV), BF16), vm((2, 16, ATT), BF16),
            pltpu.SemaphoreType.DMA((N_SEM,)), pltpu.SemaphoreType.DMA((N_SEM,)),
        ],
        compiler_params=pltpu.CompilerParams(
            collective_id=0, has_side_effects=True, vmem_limit_bytes=60 * 2**20
        ),
        cost_estimate=pl.CostEstimate(
            flops=15 * 10**9, bytes_accessed=10 * 2**20, transcendentals=2 * 10**6
        ),
    )(tokens, cotangent, cos_t, sin_t, mask, gu_in, d_in, qkv_in, out_in, jnp.asarray(pad_matrix()))
    gate_grad = from_rank(ogu[:, :, :FP])
    up_grad = from_rank(ogu[:, :, FP:])
    b_grad = lax.dynamic_slice(oqkv, (14, 18 * me), (1, 18))
    ga_grad = lax.dynamic_slice(oqkv, (15, 16 * me), (1, 14))
    gm_grad = lax.dynamic_slice(oout, (14, 14 * me), (1, 14))
    return (
        states[None], igrads[None], oqkv[None, :14], b_grad, oout[None, :14], ga_grad, gm_grad,
        gate_grad, up_grad, od[None, :76],
    )


def solution(mesh):
    return jax.shard_map(
        body,
        mesh=mesh,
        in_specs=(
            P("fsdp", None),
            P("fsdp"),
            P("fsdp", None),
            P("section", "fsdp", None),
            P("section", "fsdp"),
            P("section", "fsdp", None),
            P("section", "fsdp"),
            P("section", "fsdp"),
            P("section", "fsdp", None),
            P("section", "fsdp", None),
            P("section", "fsdp", None),
        ),
        out_specs=(
            P("section", "fsdp", None),
            P("section", "fsdp", None),
            P("section", "fsdp", None),
            P("section", "fsdp"),
            P("section", "fsdp", None),
            P("section", "fsdp"),
            P("section", "fsdp"),
            P("section", "fsdp", None),
            P("section", "fsdp", None),
            P("section", "fsdp", None),
        ),
        check_vma=False,
    )
```

time: 1490 us -> 345 us (0.23)
  local copies, waits for them, and re-layouts: 527 us -> 23 us
  waiting for transfers between devices: 439 us -> 0 us
  Pallas kernels: 0 us -> 314 us
  matrix products: 274 us -> 0 us
  blocking collectives: 182 us -> 0 us
  other arithmetic: 35.8 us -> 6.26 us
  between operations: 17.7 us -> 0.88 us
    pallas_call x0 -> x1, Pallas kernels: none -> 314 us  [body(): pl.pallas_call(kernel, out_shape=(sds((TOK, D), BF16), sds((TOK, D), F32)...]
    reduce_scatter x1 -> x0, waiting for transfers between devices: 289 us -> none  [sum_packed(): lax.psum_scatter(lines, axis, tiled=True).reshape(-1)]
    dot_general x75 -> x0, matrix products: 272 us -> none  [the longest x15 127 us: row_product(): lax.dot_general(left, right, (((0,), (0,)), ((), ())), preferred_element_...]
    unnamed x1 -> x0, blocking collectives: 182 us -> none
    unnamed x416 -> x13, local copies, waits for them, and re-layouts: 164 us -> 3.82 us
    all_gather x3 -> x0, waiting for transfers between devices: 150 us -> none  [the longest x1 150 us: sent_together(): filled = lax.all_gather(both, axis, axis=dim, tiled=True)]
    split x3 -> x0, local copies, waits for them, and re-layouts: 96.9 us -> none  [sent_together(): jnp.split(filled, [sum(widths[:k]) for k in range(1, len(widths))], axis=...]
    reshape x34 -> x4, local copies, waits for them, and re-layouts: 76.9 us -> 1.29 us  [the longest x2 0.77 us: from_rank(): pieces = grad.reshape(4, 16, 4, 4, 80)[:, :14, :, :, :76]]
  transfers between devices with their start and end apart: 8 -> 0, of which waited for: 2 -> 0; matrix products, arithmetic and copies ran while one was open for 4% -> 0% of each run, Pallas kernels for 0% -> 0%
where the time goes in v1:
time: 345 us; the launch traced here: 344 us
  Pallas kernels  314 us (91%)
  local copies, waits for them, and re-layouts  23 us (7%)
  other arithmetic  6.26 us (2%)
    pallas_call x1, Pallas kernels, body(): pl.pallas_call(kernel, out_shape=(sds((TOK, D), BF16), sds((TOK, D), F32)...  314 us

profile of v1, /device:TPU:0, one launch (start us, length us, event | category | flops | bytes accessed | tf_op | source)
XLA Modules:
  0.0 343.9 jit_solution(15862876002076289072)
XLA Ops:
  0.7 0.8 lt.40
  1.8 0.7 tile.38
  4.3 1.4 pad_maximum_fusion.1.out_in
  5.7 1.4 fusion.5.qkv_in
  7.1 1.5 fusion.4.mask
  8.6 1.0 fusion.1
  9.5 1.6 pad.17.d_in
  11.1 1.6 reshape_squeeze.6
  13.2 0.7 reshape_squeeze.7
  14.4 0.7 pad_maximum_fusion.gu_in
  15.1 313.8 %shard_map.195 = (bf16[128,896]{1,0:T(8,128)(2,1)}, f32[128,896]{1,0:T(8,128)}, bf16[4,16,2560]{2,1,0:T(8,128)(2,1)}, f32[80,896]{1,0:T(8,128)}, f32[16,1152]{1,0:T(8,128)}, /*index=5*/f32[16,896]{1,0:T(8,128)}) custom-call(bf16[128,896]{1,0:T(8,128)(2,1)} %tok.1, bf16[128,896]{1,0:T(8,128)(2,1)} %cot.1, f32[128,128]{1,0:T(8,128)} %get-tuple-element.55.cos_t, ...), custom_call_target="tpu_custom_call" | custom-call | flops 15000000512 | bytes 10485760 | tf_op jit(solution)/shard_map/pallas_call | solution.py:756
  328.9 1.3 constant_dynamic-slice_fusion.1
  330.3 1.3 constant_dynamic-slice_fusion
  331.5 1.3 constant_dynamic-slice_fusion.2
  332.8 0.8 slice_bitcast_fusion.2
  333.6 0.7 copy.41
  334.3 0.9 slice_bitcast_fusion.1
  335.2 0.7 copy.40
  335.9 1.0 slice_bitcast_fusion
  336.8 1.0 copy.42
  338.6 1.5 reshape.282
  340.9 1.5 reshape.281
  342.4 0.7 copy.49
  343.1 0.8 copy.50
  (37 shorter events, 4.6 us)
Async XLA Ops:
  0.6 12.6 %copy-start.3 = (bf16[1,14,4864]{2,1,0:T(8,128)(2,1)S(1)}, bf16[1,14,4864]{2,1,0:T(8,128)(2,1)}, u32[]{:S(2)}) copy-start(bf16[1,14,4864]{2,1,0:T(8,128)(2,1)} %param.21) | copy-start | bytes 408580
  328.9 8.9 %copy-start.1 = (bf16[4,16,2560]{2,1,0:T(8,128)(2,1)S(1)}, bf16[4,16,2560]{2,1,0:T(8,128)(2,1)}, u32[]{:S(2)}) copy-start(bf16[4,16,2560]{2,1,0:T(8,128)(2,1)} %get-tuple-element.20) | copy-start | bytes 983044
  338.6 3.8 %copy-start.2 = (bf16[128,896]{1,0:T(8,128)(2,1)S(1)}, bf16[128,896]{1,0:T(8,128)(2,1)}, u32[]{:S(2)}) copy-start(bf16[128,896]{1,0:T(8,128)(2,1)} %get-tuple-element.16) | copy-start | bytes 688132
  338.6 4.5 %copy-start = (f32[128,896]{1,0:T(8,128)S(1)}, f32[128,896]{1,0:T(8,128)}, u32[]{:S(2)}) copy-start(f32[128,896]{1,0:T(8,128)} %get-tuple-element.17) | copy-start | bytes 1376260

commit v2 on v1

v2 whole, which is shorter than its diff:
```python
import functools

import jax
import jax.numpy as jnp
import numpy as np
from jax import lax
from jax.experimental import pallas as pl
from jax.experimental.pallas import tpu as pltpu
from jax.sharding import PartitionSpec as P

D = 896
QH = 14
KVH = 2
HD = 64
FF = 4864
QKV = 1152
ROWS = 64
TOK = 128
RING = 4

DP = 1024
FP = 1280
ATT = QKV + DP
N_SEM = 160

eps_norm = 1e-06
theta_base = 1000000.0
MESH = pl.DeviceIdType.MESH
F32 = jnp.float32
BF16 = jnp.bfloat16


def dot(left, right):
    return jnp.dot(left, right, preferred_element_type=F32)


def dot_back(left, right):
    return lax.dot_general(left, right, (((1,), (1,)), ((), ())), preferred_element_type=F32)


def dot_rows(left, right):
    return lax.dot_general(left, right, (((0,), (0,)), ((), ())), preferred_element_type=F32)


def times(n, step):
    def run(i, carry):
        step(i)
        return carry

    lax.fori_loop(0, n, run, 0)


def span(start, size, unit):
    return pl.ds(pl.multiple_of(start, unit), size)


def up1(c):
    return lax.rem(c + 1, RING)


def up2(c):
    return lax.rem(c + 2, RING)


def up3(c):
    return lax.rem(c + 3, RING)


WHOLE = slice(None)
BY_AXES = (("z", "x", "y"), ("y", "z", "x"), ("x", "y", "z"))


def first_whole(index, i):
    k = index.index(WHOLE)
    return index[:k] + (i,) + index[k + 1 :]


def kernel(
    tok, cot, cos_t, sin_t, mask, gu_in, d_in, qkv_in, out_in, vec, pad_s,
    states, igrads, ogu, od, oqkv, oout, ob, oga, ogm,
    w_att, w_gu, w_d, g_out, g_qkv,
    xin, dyin, ybuf, dxbuf, h1, obuf, do_buf, datt, dp_buf, h1t, ot,
    h2all, dmall, gact, aact, dgu, h2t, at,
    part_f, part_b, sum_f, sum_b, dh,
    u1, u2, x1, proj, qs, kd, vd, probs, norms,
    gu1, gu2, gu3, gu4, d1, d2, d3, out1, out2, out3, qkv1, qkv2, qkv3,
    send, recv, turn,
):
    sec = lax.axis_index("section")
    me = lax.axis_index("fsdp")
    at_axis = {"z": me // 16, "x": lax.rem(me // 4, 4), "y": lax.rem(me, 4)}
    z, x, y = at_axis["z"], at_axis["x"], at_axis["y"]

    def device(axis, c):
        place = dict(at_axis)
        place[axis] = c
        return (sec, place["z"] * 16 + place["x"] * 4 + place["y"])

    other = (1 - sec, me)
    barrier = pltpu.get_barrier_semaphore()
    partners = [device(axis, step(at_axis[axis])) for axis in "zxy" for step in (up1, up3, up2)]
    partners.append(other)
    for dev in partners:
        pl.semaphore_signal(barrier, inc=1, device_id=dev, device_id_type=MESH)

    count = [0]
    pending = []

    def remote(src, dst, dev):
        k = count[0]
        count[0] += 1
        return pltpu.make_async_remote_copy(
            src_ref=src, dst_ref=dst, send_sem=send.at[k], recv_sem=recv.at[k],
            device_id=dev, device_id_type=MESH,
        )

    late = []

    def go(cp, pool=pending):
        cp.start()
        if not any(cp is seen for seen in pool):
            pool.append(cp)

    class RingGather:
        def __init__(self, ref, index, cols, cut, axis):
            c = at_axis[axis]
            lo, hi = cols
            whole = lambda k: ref.at[index(k) + (WHOLE, pl.ds(lo, hi - lo))]
            left = lambda k: ref.at[index(k) + (WHOLE, pl.ds(lo, cut - lo))]
            right = lambda k: ref.at[index(k) + (WHOLE, pl.ds(cut, hi - cut))]
            up, down = device(axis, up1(c)), device(axis, up3(c))
            self.a = remote(whole(c), whole(c), up)
            self.b = remote(whole(c), whole(c), down)
            self.e = remote(left(up3(c)), left(up3(c)), up)
            self.f = remote(right(up1(c)), right(up1(c)), down)

        def start(self):
            go(self.a)
            go(self.b)

        def mid(self):
            self.a.wait_recv()
            go(self.e)
            self.b.wait_recv()
            go(self.f)

        def end(self):
            self.e.wait_recv()
            self.f.wait_recv()

    class Gather:
        def __init__(self, ref, index, cols, axis):
            c = at_axis[axis]
            block = ref.at[index(c) + (WHOLE, pl.ds(cols[0], cols[1] - cols[0]))]
            self.copies = [remote(block, block, device(axis, step(c))) for step in (up1, up3, up2)]

        def start(self):
            for cp in self.copies:
                go(cp)

        def end(self):
            for cp in self.copies:
                cp.wait_recv()

    class RingReduce:
        def __init__(self, ref, index, cols, axis, r1, r2):
            c = at_axis[axis]
            lo, hi = cols
            cut = (lo + hi) // 2
            self.ref, self.index, self.c, self.r1, self.r2 = ref, index, c, r1, r2
            self.whole = pl.ds(lo, hi - lo)
            self.left, self.right = pl.ds(lo, cut - lo), pl.ds(cut, hi - cut)
            view = lambda k, part: ref.at[index(k) + (WHOLE, part)]
            up, down = device(axis, up1(c)), device(axis, up3(c))
            self.a = remote(view(up2(c), self.left), r1.at[0], up)
            self.b = remote(view(up2(c), self.right), r1.at[1], down)
            self.e = remote(view(up1(c), self.whole), r2.at[0], up)
            self.f = remote(view(up3(c), self.whole), r2.at[1], down)

        def start(self):
            go(self.a)
            go(self.b)

        def add(self, k, cols, slot):
            def step(i):
                here = first_whole(self.index(k), i) + (WHOLE, cols)
                self.ref[here] = (
                    self.ref[here].astype(F32) + self.r1[slot, i].astype(F32)).astype(BF16)

            times(RING, step)

        def mid(self):
            self.a.wait_recv()
            self.add(up1(self.c), self.left, 0)
            go(self.e)
            self.b.wait_recv()
            self.add(up3(self.c), self.right, 1)
            go(self.f)

        def end(self):
            self.e.wait_recv()
            self.f.wait_recv()

            def step(i):
                here = first_whole(self.index(self.c), i) + (WHOLE, self.whole)
                self.ref[here] = (
                    self.ref[here].astype(F32) + self.r2[0, i].astype(F32) + self.r2[1, i].astype(F32)
                ).astype(BF16)

            times(RING, step)

    class Reduce:
        def __init__(self, ref, index, cols, axis, r):
            c = at_axis[axis]
            part = pl.ds(cols[0], cols[1] - cols[0])
            self.ref, self.r, self.here = ref, r, index(c) + (WHOLE, part)
            self.copies = [
                remote(ref.at[index(step(c)) + (WHOLE, part)], r.at[k], device(axis, step(c)))
                for k, step in enumerate((up1, up3, up2))
            ]

        def start(self):
            for cp in self.copies:
                go(cp)

        def total(self):
            for cp in self.copies:
                cp.wait_recv()
            return self.ref[self.here].astype(F32) + (
                self.r[0].astype(F32) + self.r[1].astype(F32) + self.r[2].astype(F32))

        def end(self):
            self.ref[self.here] = self.total().astype(BF16)

    class TokenGather:
        def __init__(self, ref, pool):
            self.pool = pool
            up, down = device("y", up1(y)), device("y", up3(y))
            self.a = remote(ref.at[0], ref.at[1], up)
            self.b = remote(ref.at[0], ref.at[2], down)
            left, right = pl.ds(0, 512), pl.ds(512, 512)
            self.e = remote(ref.at[1, :, left], ref.at[3, :, left], up)
            self.f = remote(ref.at[2, :, right], ref.at[3, :, right], down)

        def start(self):
            go(self.a, self.pool)
            go(self.b, self.pool)

        def mid(self):
            self.a.wait_recv()
            go(self.e, self.pool)
            self.b.wait_recv()
            go(self.f, self.pool)

        def end(self):
            self.e.wait_recv()
            self.f.wait_recv()

    def gathered(order, phase):
        done = order[:phase]
        return lambda c: tuple(
            WHOLE if a in done else c if a == order[phase] else at_axis[a] for a in ("z", "x", "y"))

    def reduced(order, phase):
        done = order[:phase]
        return lambda c: tuple(
            at_axis[a] if a in done else c if a == order[phase] else WHOLE for a in ("z", "x", "y"))

    mine = pl.ds(pl.multiple_of(16 * y, 16), 16)

    to_rank = [
        remote(gu_in.at[step(y)], w_gu.at[z, x, mine], device("y", step(y))) for step in (up1, up3, up2)]
    gate_x = Gather(w_gu, lambda c: (z, c), (0, FP), "x")
    gate_z = RingGather(w_gu, lambda c: (c, WHOLE), (0, FP), FP // 2, "z")
    up_z = Gather(w_gu, lambda c: (c, x), (FP, 2 * FP), "z")
    up_x = RingGather(w_gu, lambda c: (WHOLE, c), (FP, 2 * FP), FP + FP // 2, "x")
    low_x = Gather(w_d, lambda c: (c, z), (0, 512), "x")
    low_z = RingGather(w_d, lambda c: (WHOLE, c), (0, 512), 256, "z")
    high_z = Gather(w_d, lambda c: (x, c), (512, DP), "z")
    high_x = RingGather(w_d, lambda c: (c, WHOLE), (512, DP), 768, "x")
    att_cols = ((0, QKV), (QKV, QKV + 512), (QKV + 512, ATT))
    att_cut = (640, QKV + 256, QKV + 768)
    att_0 = [Gather(w_att, gathered(o, 0), c, o[0]) for o, c in zip(BY_AXES, att_cols)]
    att_1 = [Gather(w_att, gathered(o, 1), c, o[1]) for o, c in zip(BY_AXES, att_cols)]
    att_2 = [
        RingGather(w_att, gathered(o, 2), c, k, o[2]) for o, c, k in zip(BY_AXES, att_cols, att_cut)]

    pl.semaphore_wait(barrier, len(partners))
    for cp in to_rank:
        go(cp)

    w_gu[z, x, mine, :] = gu_in[y]

    def placed(n, width):
        source = lax.broadcasted_iota(jnp.int32, (128, width), 0)
        target = lax.broadcasted_iota(jnp.int32, (128, width), 1)
        return jnp.where((target == source + n * me) & (source < n), 1.0, 0.0).astype(BF16)

    x1[0:76, pl.ds(0, D)] = d_in[...].astype(F32)
    x1[76:80, pl.ds(0, D)] = jnp.zeros((4, D), F32)
    w_d[x, z] = dot(x1[0:80, pl.ds(0, D)].astype(BF16), pad_s[...]).astype(BF16)
    bias = dot(vec[...], placed(18, QKV))
    gains = dot(vec[...], placed(14, D))
    proj[0:14, :] = qkv_in[...].astype(F32)
    proj[14:15, :] = bias[0:1]
    proj[15:16, pl.ds(0, D)] = gains[1:2]
    proj[15:16, pl.ds(D, QKV - D)] = jnp.zeros((1, QKV - D), F32)
    w_att[z, x, y, :, :QKV] = proj[0:16, :].astype(BF16)
    u1[0:14, pl.ds(0, D)] = out_in[...].astype(F32)
    u1[14:15, pl.ds(0, D)] = gains[2:3]
    u1[15:16, pl.ds(0, D)] = jnp.zeros((1, D), F32)
    w_att[z, x, y, :, QKV:] = dot(u1[0:16, pl.ds(0, D)].astype(BF16), pad_s[...]).astype(BF16)

    for g in att_0:
        g.start()
    low_x.start()
    high_z.start()
    for cp in to_rank:
        cp.wait_recv()

    @pl.when(sec == 1)
    def _():
        pl.semaphore_wait(turn, 1)

    gate_x.start()
    up_z.start()
    for g, after in zip(att_0, att_1):
        g.end()
        after.start()
    low_x.end()
    high_z.end()
    for g, after in zip(att_1, att_2):
        g.end()
        after.start()
    gate_x.end()
    gate_z.start()
    up_z.end()
    up_x.start()
    low_z.start()
    high_x.start()
    for g in att_2:
        g.mid()
    gate_z.mid()
    up_x.mid()

    @pl.when(sec == 0)
    def _():
        pl.semaphore_signal(turn, inc=1, device_id=other, device_id_type=MESH)

    att_2[0].end()

    send_y = remote(ybuf, xin, other)
    send_dx = remote(dxbuf, dyin, other)
    dmg = TokenGather(dmall, late)

    @pl.when(sec == 0)
    def _():
        xin[...] = dot(tok[...], pad_s[...]).astype(BF16)

    @pl.when(sec == 1)
    def _():
        dyin[...] = dot(cot[...], pad_s[...]).astype(BF16)
        dmall[0] = dyin[...]
        dmg.start()
        send_y.wait_recv()

    lanes = lax.broadcasted_iota(jnp.int32, (TOK, DP), 1)
    slot = lax.rem(lanes, 16)
    picks = lax.rem(lax.broadcasted_iota(jnp.int32, (8, DP), 1), 16)
    pick15 = jnp.where(picks == 15, 1.0, 0.0).astype(BF16)
    pick14 = jnp.where(picks == 14, 1.0, 0.0).astype(BF16)
    lane = lax.broadcasted_iota(jnp.int32, (TOK, 128), 1)
    low_half = lane < HD
    first = lax.rem(lane, HD) < HD // 2

    def att_weight(start, size):
        return w_att[:, :, :, :, pl.ds(start, size)].reshape(DP, size)

    def swap(tile):
        return jnp.where(first, pltpu.roll(tile, 96, 1), pltpu.roll(tile, 32, 1))

    stream = xin[...].astype(F32)
    inv1 = lax.rsqrt(jnp.sum(stream * stream, axis=1, keepdims=True) * (1.0 / D) + eps_norm)
    norms[0] = inv1
    gains = dot(pick15, att_weight(0, D)).astype(BF16)
    gain_a = dot(gains, pad_s[...])[0:1]
    unit1 = stream * inv1
    u1[...] = unit1
    h1[...] = jnp.where(slot == 14, 1.0, unit1 * gain_a).astype(BF16)
    for i in range(3):
        proj[:, pl.ds(384 * i, 384)] = dot(h1[...], att_weight(384 * i, 384))

    def rotated(j):
        tile = proj[:, pl.ds(128 * j, 128)]
        return tile * cos_t[...] + swap(tile) * sin_t[...]

    def both(tile):
        rolled = pltpu.roll(tile, HD, 1)
        return (
            jnp.where(low_half, tile, rolled).astype(BF16),
            jnp.where(low_half, rolled, tile).astype(BF16),
        )

    def keep(head):
        return low_half if head % 2 == 0 else ~low_half

    kd[0], kd[1] = both(rotated(7))
    vd[0], vd[1] = both(proj[:, pl.ds(1024, 128)])
    allowed = mask[...] > 0.5
    for t in range(7):
        tile = rotated(t)
        outs = []
        for head in (2 * t, 2 * t + 1):
            kv = head // 7
            q = jnp.where(keep(head), tile, 0.0).astype(BF16)
            qs[head] = q
            s = dot_back(q, kd[kv]) * HD ** (-0.5)
            s = jnp.where(allowed, s, -1e30)
            weights = jnp.exp(s - jnp.max(s, axis=1, keepdims=True))
            pr = weights / jnp.sum(weights, axis=1, keepdims=True)
            probs[head] = pr
            outs.append(dot(pr.astype(BF16), vd[kv]))
        dp_buf[:, pl.ds(128 * t, 128)] = jnp.where(low_half, outs[0], outs[1]).astype(BF16)
    obuf[...] = dot(dp_buf[:, pl.ds(0, D)], pad_s[...]).astype(BF16)
    att_2[1].end()
    att_2[2].end()
    gain_m = dot(pick14, att_weight(QKV, DP))[0:1]
    for i in range(4):
        cols = pl.ds(256 * i, 256)
        x1[:, cols] = xin[:, cols].astype(F32) + dot(obuf[...], att_weight(QKV + 256 * i, 256))
    middle = x1[...]
    inv2 = lax.rsqrt(jnp.sum(middle * middle, axis=1, keepdims=True) * (1.0 / D) + eps_norm)
    norms[1] = inv2
    unit2 = middle * inv2
    u2[...] = unit2
    h2all[0] = (unit2 * gain_m).astype(BF16)

    def token_sums(part, sums):
        return [
            remote(part.at[1], sums.at[0], device("y", up3(y))),
            remote(part.at[2], sums.at[1], device("y", up1(y))),
            remote(part.at[3], sums.at[2], device("y", up2(y))),
        ]

    def token_total(part, sums, copies):
        for cp in copies:
            cp.wait_recv()
        return part[0].astype(F32) + (
            sums[0].astype(F32) + sums[1].astype(F32) + sums[2].astype(F32))

    def mlp(k, n):
        rows = n * TOK
        for i in range(5):
            cols, cols_up = pl.ds(256 * i, 256), pl.ds(FP + 256 * i, 256)
            h = h2all[k : k + n].reshape(rows, DP)
            gate = dot(h, w_gu[:, :, :, cols].reshape(DP, 256))
            upward = dot(h, w_gu[:, :, :, cols_up].reshape(DP, 256))
            gact[k : k + n, :, cols] = gate.reshape(n, TOK, 256)
            gact[k : k + n, :, cols_up] = upward.reshape(n, TOK, 256)
            aact[k : k + n, :, cols] = (
                gate * jax.nn.sigmoid(gate) * upward).astype(BF16).reshape(n, TOK, 256)
        for i in range(4):
            cols = pl.ds(256 * i, 256)
            a = aact[k : k + n].reshape(rows, FP)
            part_f[k : k + n, :, cols] = dot(
                a, w_d[:, :, :, cols].reshape(FP, 256)).astype(BF16).reshape(n, TOK, 256)

    ag = TokenGather(h2all, pending)
    sums = token_sums(part_f, sum_f)
    ag.start()

    @pl.when(sec == 1)
    def _():
        dmg.mid()

    gate_z.end()
    up_x.end()
    low_z.mid()
    high_x.mid()
    low_z.end()
    high_x.end()

    mlp(0, 1)
    ag.mid()
    mlp(1, 2)
    go(sums[0])
    go(sums[1])
    ag.end()
    mlp(3, 1)
    go(sums[2])
    for c in range(RING):
        cols = pl.ds(128 * c, 128)
        h2t[:, cols] = h2all[c].T
        at[:, cols] = aact[c].T
    h1t[...] = h1[...].T
    ot[...] = obuf[...].T
    out = x1[...] + token_total(part_f, sum_f, sums)
    for cp in pending:
        cp.wait_send()
    pending.clear()
    ybuf[...] = out.astype(BF16)

    @pl.when(sec == 0)
    def _():
        send_y.start()


    def store_states():
        states[...] = dot_back(ybuf[...], pad_s[...]).astype(BF16)

    @pl.when(sec == 0)
    def _():
        store_states()
        send_dx.wait_recv()
        dmall[0] = dyin[...]
        dmg.start()

    def mlp_back(k, n):
        rows = n * TOK
        for i in range(2):
            cols, cols_up = pl.ds(640 * i, 640), pl.ds(FP + 640 * i, 640)
            da = dot_back(dmall[k : k + n].reshape(rows, DP), w_d[2 * i : 2 * i + 2].reshape(640, DP))
            gate = gact[k : k + n, :, cols].reshape(rows, 640)
            upward = gact[k : k + n, :, cols_up].reshape(rows, 640)
            sig = jax.nn.sigmoid(gate)
            dgate = da * upward * (sig * (1.0 + gate * (1.0 - sig)))
            dgu[k : k + n, :, cols] = dgate.astype(BF16).reshape(n, TOK, 640)
            dgu[k : k + n, :, cols_up] = (da * gate * sig).astype(BF16).reshape(n, TOK, 640)
        for i in range(4):
            cols = pl.ds(256 * i, 256)
            part_b[k : k + n, :, cols] = dot_back(
                dgu[k : k + n].reshape(rows, 2 * FP), w_gu[i].reshape(256, 2 * FP)
            ).astype(BF16).reshape(n, TOK, 256)

    sums = token_sums(part_b, sum_b)
    mlp_back(0, 1)

    @pl.when(sec == 0)
    def _():
        dmg.mid()

    mlp_back(1, 2)
    go(sums[0])
    go(sums[1])
    dmg.end()
    mlp_back(3, 1)
    go(sums[2])

    rgate_z = RingReduce(w_gu, lambda c: (c, WHOLE), (0, FP), "z", gu1.at[0], gu2.at[0])
    rup_x = RingReduce(w_gu, lambda c: (WHOLE, c), (FP, 2 * FP), "x", gu1.at[1], gu2.at[1])
    rgate_x = Reduce(w_gu, lambda c: (z, c), (0, FP), "x", gu3.at[0])
    rup_z = Reduce(w_gu, lambda c: (c, x), (FP, 2 * FP), "z", gu3.at[1])
    rlow_z = RingReduce(w_d, lambda c: (WHOLE, c), (0, 512), "z", d1.at[0], d2.at[0])
    rhigh_x = RingReduce(w_d, lambda c: (c, WHOLE), (512, DP), "x", d1.at[1], d2.at[1])
    rlow_x = Reduce(w_d, lambda c: (c, z), (0, 512), "x", d3.at[0])
    rhigh_z = Reduce(w_d, lambda c: (x, c), (512, DP), "z", d3.at[1])
    from_rank = [
        remote(
            w_gu.at[z, x, pl.ds(pl.multiple_of(16 * step(y), 16), 16)],
            gu4.at[y], device("y", step(y)))
        for step in (up1, up3, up2)
    ]
    out_red = [
        Reduce(g_out, reduced("yxz", k), (0, DP), "yxz"[k], r) for k, r in enumerate((out1, out2, out3))]
    qkv_order = ("yxz", "xzy", "zyx")
    qkv_red = [
        [
            Reduce(g_qkv, reduced(order, k), (384 * n, 384 * n + 384), order[k], r.at[n])
            for n, order in enumerate(qkv_order)
        ]
        for k, r in enumerate((qkv1, qkv2, qkv3))
    ]

    def gu_terms():
        def grad_gate(i):
            rows = span(256 * i, 256, 256)
            g = dot(h2t[rows, :], dgu[:, :, pl.ds(0, FP)].reshape(512, FP))
            w_gu[i, :, :, pl.ds(0, FP)] = g.astype(BF16).reshape(4, 64, FP)

        def grad_up(i):
            rows = span(256 * i, 256, 256)
            g = dot(h2t[rows, :], dgu[:, :, pl.ds(FP, FP)].reshape(512, FP))
            w_gu[i, :, :, pl.ds(FP, FP)] = g.astype(BF16).reshape(4, 64, FP)

        times(4, grad_gate)
        rgate_z.start()
        times(4, grad_up)
        rup_x.start()

    def d_terms():
        def grad_d(i):
            rows = span(320 * i, 320, 64)
            g = dot(at[rows, :], dmall[...].reshape(512, DP))
            w_d[i] = g.astype(BF16).reshape(4, 80, DP)

        times(4, grad_d)
        rlow_z.start()
        rhigh_x.start()

    row = lax.rem(lax.broadcasted_iota(jnp.int32, (256, 384), 0), 16)

    def out_terms():
        def grad(i):
            g = dot(ot[span(256 * i, 256, 256), :], datt[...])
            g = jnp.where(row14, dh[0:1, :], g)
            g_out[i] = g.astype(BF16).reshape(4, 4, 16, DP)

        row14 = lax.rem(lax.broadcasted_iota(jnp.int32, (256, DP), 0), 16) == 14
        times(4, grad)
        out_red[0].start()

    gu_terms()

    @pl.when(sec == 0)
    def _():
        d_terms()

    dh2 = token_total(part_b, sum_b, sums)
    unit2 = u2[...]
    dh[0:1, :] = jnp.sum(dh2 * unit2, axis=0, keepdims=True)
    gained = dh2 * gain_m
    dx1 = dyin[...].astype(F32) + norms[1] * (
        gained - unit2 * (jnp.sum(gained * unit2, axis=1, keepdims=True) * (1.0 / D)))
    x1[...] = dx1
    datt[...] = dx1.astype(BF16)

    @pl.when(sec == 0)
    def _():
        out_terms()

    for i in range(4):
        w = w_att[i, :, :, :, pl.ds(QKV, DP)].reshape(256, DP)
        do_buf[:, pl.ds(256 * i, 256)] = dot_back(datt[...], w).astype(BF16)
    proj[:, pl.ds(0, D)] = dot_back(do_buf[...], pad_s[...])

    def unrotated(tile):
        return (tile * cos_t[...] - swap(tile) * sin_t[...]).astype(BF16)

    dk_sum = [jnp.zeros((TOK, 128), F32)] * 2
    dv_sum = [jnp.zeros((TOK, 128), F32)] * 2
    for t in range(7):
        tile = proj[:, pl.ds(128 * t, 128)]
        dqs = []
        for head in (2 * t, 2 * t + 1):
            kv = head // 7
            do_h = jnp.where(keep(head), tile, 0.0).astype(BF16)
            pr = probs[head]
            dpr = dot_back(do_h, vd[kv])
            ds = (pr * (dpr - jnp.sum(dpr * pr, axis=1, keepdims=True))).astype(BF16)
            dv_sum[kv] = dv_sum[kv] + dot_rows(pr.astype(BF16), do_h)
            dk_sum[kv] = dk_sum[kv] + dot_rows(ds, qs[head])
            dqs.append(dot(ds, kd[kv]) * HD ** (-0.5))
        dp_buf[:, pl.ds(128 * t, 128)] = unrotated(jnp.where(low_half, dqs[0], dqs[1]))
    dk_sum = [(dk + pltpu.roll(dk, HD, 1)) * HD ** (-0.5) for dk in dk_sum]
    dv_sum = [dv + pltpu.roll(dv, HD, 1) for dv in dv_sum]
    dp_buf[:, pl.ds(896, 128)] = unrotated(jnp.where(low_half, dk_sum[0], dk_sum[1]))
    dp_buf[:, pl.ds(1024, 128)] = jnp.where(low_half, dv_sum[0], dv_sum[1]).astype(BF16)
    rgate_z.mid()
    rup_x.mid()
    for i in range(4):
        w = w_att[i, :, :, :, pl.ds(0, QKV)].reshape(256, QKV)
        proj[:, pl.ds(256 * i, 256)] = dot_back(dp_buf[...], w)
    dh1 = jnp.where(slot < 14, proj[:, pl.ds(0, DP)], 0.0)
    unit1 = u1[...]
    dgain_a = jnp.sum(dh1 * unit1, axis=0, keepdims=True)

    def qkv_terms():
        proj[0:1, pl.ds(0, DP)] = dgain_a
        for n in range(3):
            cols = pl.ds(384 * n, 384)

            def grad(i, cols=cols):
                g = dot(h1t[span(256 * i, 256, 256), :], dp_buf[:, cols])
                g = jnp.where(row == 15, proj[0:1, cols], g)
                g_qkv[i, :, :, :, cols] = g.astype(BF16).reshape(4, 4, 16, 384)

            times(4, grad)
            qkv_red[0][n].start()

    @pl.when(sec == 0)
    def _():
        qkv_terms()

    gained = dh1 * gain_a
    dx = x1[...] + norms[0] * (
        gained - unit1 * (jnp.sum(gained * unit1, axis=1, keepdims=True) * (1.0 / D)))
    dx_hi = dx.astype(BF16)
    dxbuf[...] = dx_hi

    @pl.when(sec == 1)
    def _():
        send_dx.start()
        igrads[...] = dot_back(dx_hi, pad_s[...])
        d_terms()
        out_terms()
        qkv_terms()
        store_states()

    @pl.when(sec == 0)
    def _():
        dx_lo = (dx - dx_hi.astype(F32)).astype(BF16)
        igrads[...] = dot_back(dx_hi, pad_s[...]) + dot_back(dx_lo, pad_s[...])

    rlow_z.mid()
    rhigh_x.mid()
    out_red[0].end()
    out_red[1].start()
    rgate_z.end()
    rgate_x.start()
    rup_x.end()
    rup_z.start()
    for red, after in zip(qkv_red[0], qkv_red[1]):
        red.end()
        after.start()
    rlow_z.end()
    rlow_x.start()
    rhigh_x.end()
    rhigh_z.start()
    out_red[1].end()
    out_red[2].start()
    rgate_x.end()
    rup_z.end()
    for cp in from_rank:
        go(cp)
    for red, after in zip(qkv_red[1], qkv_red[2]):
        red.end()
        after.start()

    def unpadded(total):
        hi = total.astype(BF16)
        lo = (total - hi.astype(F32)).astype(BF16)
        return dot_back(hi, pad_s[...]) + dot_back(lo, pad_s[...])

    def own_lanes(rows, n):
        width = rows.shape[1]
        target = lax.broadcasted_iota(jnp.int32, (width, 128), 1)
        source = lax.broadcasted_iota(jnp.int32, (width, 128), 0)
        move = jnp.where(source == target + n * me, 1.0, 0.0).astype(BF16)
        hi = rows.astype(BF16)
        lo = (rows - hi.astype(F32)).astype(BF16)
        return dot(hi, move) + dot(lo, move)

    od[...] = unpadded(jnp.concatenate([rlow_x.total(), rhigh_z.total()], axis=1))[0:76]
    total = unpadded(out_red[2].total())
    oout[...] = total[0:14]
    ogm[...] = own_lanes(total, 14)[14:15, 0:14]
    for n in range(3):
        proj[0:16, pl.ds(384 * n, 384)] = qkv_red[2][n].total()
    oqkv[...] = proj[0:14, :]
    ob[...] = own_lanes(proj[0:16, :], 18)[14:15, 0:18]
    oga[...] = own_lanes(proj[0:16, pl.ds(0, DP)], 16)[15:16, 0:14]
    ogu[y] = w_gu[z, x, mine, :]
    for cp in from_rank:
        cp.wait_recv()
    for step in (up1, up3, up2):
        ogu[step(y)] = gu4[step(y)]

    for cp in pending + late:
        cp.wait_send()

    @pl.when(sec == 0)
    def _():
        send_y.wait_send()

    @pl.when(sec == 1)
    def _():
        send_dx.wait_send()


def pad_matrix():
    column = np.arange(DP)
    row = np.where(column % 16 < 14, 14 * (column // 16) + column % 16, -1)
    return (np.arange(D)[:, None] == row[None, :]).astype(jnp.bfloat16)


def tables(segments):
    seg = segments.reshape(TOK // ROWS, ROWS)
    earlier = jnp.sum((seg[:, None, :] < seg[:, :, None]).astype(jnp.int32), axis=2)
    place = (jnp.arange(ROWS, dtype=jnp.int32)[None] - earlier).astype(F32).reshape(TOK)
    half = HD // 2
    inverse = theta_base ** (-(jnp.arange(half, dtype=F32) * 2.0 / HD))
    angles = place[:, None] * jnp.tile(inverse, 4)[None, :]
    sign = jnp.where(jnp.arange(128) % HD < half, -1.0, 1.0).astype(F32)
    index = jnp.arange(TOK)
    allowed = (
        (segments[:, None] == segments[None, :])
        & (index[None, :] <= index[:, None])
        & (index[None, :] // ROWS == index[:, None] // ROWS)
    )
    return jnp.cos(angles), jnp.sin(angles) * sign, allowed.astype(F32)


def by_rank(weight):
    pieces = weight.reshape(14, 4, 4, 4, 76).transpose(3, 0, 2, 1, 4)
    return jnp.pad(pieces, ((0, 0), (0, 2), (0, 0), (0, 0), (0, 4))).reshape(4, 16, FP)


def from_rank(grad):
    pieces = grad.reshape(4, 16, 4, 4, 80)[:, :14, :, :, :76]
    return pieces.transpose(1, 3, 2, 0, 4).reshape(1, 14, FF).astype(F32)


def body(
    tokens, segments, cotangent, w_qkv, b_qkv, w_out, gain_attn, gain_mlp, w_gate, w_up, w_down
):
    cos_t, sin_t, mask = tables(segments)
    gu_in = jnp.concatenate([by_rank(w_gate[0]), by_rank(w_up[0])], axis=2)
    vec = jnp.concatenate(
        [jnp.pad(v, ((0, 0), (0, 128 - v.shape[1]))) for v in (b_qkv, gain_attn, gain_mlp)])
    vec = jnp.pad(vec, ((0, 13), (0, 0)))
    sds = jax.ShapeDtypeStruct
    vm = pltpu.VMEM
    states, igrads, ogu, od, oqkv, oout, b_grad, ga_grad, gm_grad = pl.pallas_call(
        kernel,
        out_shape=(
            sds((TOK, D), BF16), sds((TOK, D), F32), sds((4, 16, 2 * FP), BF16),
            sds((76, D), F32), sds((14, QKV), F32), sds((14, D), F32),
            sds((1, 18), F32), sds((1, 14), F32), sds((1, 14), F32),
        ),
        in_specs=[pl.BlockSpec(memory_space=pltpu.VMEM)] * 11,
        out_specs=tuple([pl.BlockSpec(memory_space=pltpu.VMEM)] * 9),
        scratch_shapes=[
            vm((4, 4, 4, 16, ATT), BF16), vm((4, 4, 64, 2 * FP), BF16), vm((4, 4, 80, DP), BF16),
            vm((4, 4, 4, 16, DP), BF16), vm((4, 4, 4, 16, QKV), BF16),
            *[vm((TOK, DP), BF16)] * 8, vm((TOK, QKV), BF16), vm((DP, TOK), BF16), vm((DP, TOK), BF16),
            vm((4, TOK, DP), BF16), vm((4, TOK, DP), BF16), vm((4, TOK, 2 * FP), F32),
            vm((4, TOK, FP), BF16), vm((4, TOK, 2 * FP), BF16), vm((DP, 512), BF16), vm((FP, 512), BF16),
            vm((4, TOK, DP), BF16), vm((4, TOK, DP), BF16),
            vm((3, TOK, DP), BF16), vm((3, TOK, DP), BF16), vm((8, DP), F32),
            vm((TOK, DP), F32), vm((TOK, DP), F32), vm((TOK, DP), F32), vm((TOK, QKV), F32),
            vm((QH, TOK, 128), BF16), vm((2, TOK, 128), BF16), vm((2, TOK, 128), BF16),
            vm((QH, TOK, 128), F32), vm((2, TOK, 1), F32),
            vm((2, 2, 4, 64, FP // 2), BF16), vm((2, 2, 4, 64, FP), BF16),
            vm((2, 3, 64, FP), BF16), vm((4, 16, 2 * FP), BF16),
            vm((2, 2, 4, 80, 256), BF16), vm((2, 2, 4, 80, 512), BF16), vm((2, 3, 80, 512), BF16),
            vm((3, 4, 4, 16, DP), BF16), vm((3, 4, 16, DP), BF16), vm((3, 16, DP), BF16),
            vm((3, 3, 4, 4, 16, 384), BF16), vm((3, 3, 4, 16, 384), BF16), vm((3, 3, 16, 384), BF16),
            pltpu.SemaphoreType.DMA((N_SEM,)), pltpu.SemaphoreType.DMA((N_SEM,)),
            pltpu.SemaphoreType.REGULAR,
        ],
        compiler_params=pltpu.CompilerParams(
            collective_id=0, has_side_effects=True, vmem_limit_bytes=60 * 2**20
        ),
        cost_estimate=pl.CostEstimate(
            flops=15 * 10**9, bytes_accessed=10 * 2**20, transcendentals=2 * 10**6
        ),
    )(
        tokens, cotangent, cos_t, sin_t, mask, gu_in, w_down[0], w_qkv[0], w_out[0], vec,
        jnp.asarray(pad_matrix()),
    )
    return (
        states[None], igrads[None], oqkv[None], b_grad, oout[None], ga_grad, gm_grad,
        from_rank(ogu[:, :, :FP]), from_rank(ogu[:, :, FP:]), od[None],
    )


def solution(mesh):
    return jax.shard_map(
        body,
        mesh=mesh,
        in_specs=(
            P("fsdp", None),
            P("fsdp"),
            P("fsdp", None),
            P("section", "fsdp", None),
            P("section", "fsdp"),
            P("section", "fsdp", None),
            P("section", "fsdp"),
            P("section", "fsdp"),
            P("section", "fsdp", None),
            P("section", "fsdp", None),
            P("section", "fsdp", None),
        ),
        out_specs=(
            P("section", "fsdp", None),
            P("section", "fsdp", None),
            P("section", "fsdp", None),
            P("section", "fsdp"),
            P("section", "fsdp", None),
            P("section", "fsdp"),
            P("section", "fsdp"),
            P("section", "fsdp", None),
            P("section", "fsdp", None),
            P("section", "fsdp", None),
        ),
        check_vma=False,
    )
```

time: 345 us -> 214 us (0.62)
  Pallas kernels: 314 us -> 190 us
  local copies, waits for them, and re-layouts: 23 us -> 18.2 us
    pallas_call x1, Pallas kernels: 314 us -> 190 us  [body(): pl.pallas_call(kernel, out_shape=(sds((TOK, D), BF16), sds((TOK, D), F32)...]
    unnamed x13 -> x20, local copies, waits for them, and re-layouts: 3.82 us -> 8.02 us
    dynamic_slice x3 -> x0, local copies, waits for them, and re-layouts: 3.86 us -> none  [the longest x1 1.33 us: body(): gm_grad = lax.dynamic_slice(oout, (14, 14 * me), (1, 14))]
where the time goes in v2:
time: 214 us
  Pallas kernels  190 us (89%)
  local copies, waits for them, and re-layouts  18.2 us (9%)
  other arithmetic  4.18 us (2%)
    pallas_call x1, Pallas kernels, body(): pl.pallas_call(kernel, out_shape=(sds((TOK, D), BF16), sds((TOK, D), F32)...  190 us
    unnamed x20, local copies, waits for them, and re-layouts  8.02 us

profile of v2, /device:TPU:0, one launch (start us, length us, event | category | flops | bytes accessed | tf_op | source)
XLA Modules:
  0.0 213.7 jit_solution(645722699216179304)
XLA Ops:
  0.7 0.7 fusion.9
  1.4 0.7 lt.31
  2.5 0.6 pad.27.vec
  3.1 1.5 fusion.3.mask
  4.6 1.0 fusion
  5.6 1.6 reshape_squeeze.6
  7.6 0.7 reshape_squeeze.7
  8.8 0.7 pad_maximum_fusion.gu_in
  9.6 190.4 %shard_map.195 = (bf16[128,896]{1,0:T(8,128)(2,1)}, f32[128,896]{1,0:T(8,128)}, bf16[4,16,2560]{2,1,0:T(8,128)(2,1)}, f32[76,896]{1,0:T(8,128)}, f32[14,1152]{1,...) custom-call(bf16[128,896]{1,0:T(8,128)(2,1)} %tok.1, ...), custom_call_target="tpu_custom_call" | custom-call | flops 15000000512 | bytes 10485760 | tf_op jit(solution)/shard_map/pallas_call | solution.py:813
  200.0 1.5 copy.34
  201.5 1.6 copy.33
  203.1 1.9 copy.35
  205.0 1.0 fusion.10
  206.1 0.4 reshape.175
  206.5 0.3 copy.32
  206.8 1.5 reshape.177
  208.4 0.4 reshape.174
  208.8 0.3 copy.31
  209.1 1.5 reshape.176
  210.7 0.7 copy.45
  211.4 0.8 copy.46
  212.1 0.5 copy.47
  212.7 0.5 copy.48
  213.2 0.5 copy.49
  (28 shorter events, 1.4 us)
Async XLA Ops:
  0.6 7.0 %copy-start.2 = (bf16[1,14,4864]{2,1,0:T(8,128)(2,1)S(1)}, bf16[1,14,4864]{2,1,0:T(8,128)(2,1)}, u32[]{:S(2)}) copy-start(bf16[1,14,4864]{2,1,0:T(8,128)(2,1)} %param.21) | copy-start | bytes 408580
  206.8 3.9 %copy-start.1 = (bf16[128,896]{1,0:T(8,128)(2,1)S(1)}, bf16[128,896]{1,0:T(8,128)(2,1)}, u32[]{:S(2)}) copy-start(bf16[128,896]{1,0:T(8,128)(2,1)} %get-tuple-element.19) | copy-start | bytes 688132
  206.8 4.6 %copy-start = (f32[128,896]{1,0:T(8,128)S(1)}, f32[128,896]{1,0:T(8,128)}, u32[]{:S(2)}) copy-start(f32[128,896]{1,0:T(8,128)} %get-tuple-element.20) | copy-start | bytes 1376260
  208.8 3.4 %copy-start.5 = (f32[1,18]{1,0:T(1,128)S(1)}, f32[1,18]{1,0:T(1,128)}, u32[]{:S(2)}) copy-start(f32[1,18]{1,0:T(1,128)} %get-tuple-element.65) | copy-start | bytes 220
  208.8 3.9 %copy-start.4 = (f32[1,14]{1,0:T(1,128)S(1)}, f32[1,14]{1,0:T(1,128)}, u32[]{:S(2)}) copy-start(f32[1,14]{1,0:T(1,128)} %get-tuple-element.67) | copy-start | bytes 172
  208.8 4.4 %copy-start.3 = (f32[1,14]{1,0:T(1,128)S(1)}, f32[1,14]{1,0:T(1,128)}, u32[]{:S(2)}) copy-start(f32[1,14]{1,0:T(1,128)} %get-tuple-element.68) | copy-start | bytes 172

commit v3 on v2

--- a/solution.py
+++ b/solution.py
@@ -76,7 +76,7 @@
 
 
 def kernel(
-    tok, cot, cos_t, sin_t, mask, gu_in, d_in, qkv_in, out_in, vec, pad_s,
+    tok, cot, seg, freq, gu_in, d_in, qkv_in, out_in, vec, pad_s,
     states, igrads, ogu, od, oqkv, oout, ob, oga, ogm,
     w_att, w_gu, w_d, g_out, g_qkv,
     xin, dyin, ybuf, dxbuf, h1, obuf, do_buf, datt, dp_buf, h1t, ot,
@@ -84,7 +84,7 @@
     part_f, part_b, sum_f, sum_b, dh,
     u1, u2, x1, proj, qs, kd, vd, probs, norms,
     gu1, gu2, gu3, gu4, d1, d2, d3, out1, out2, out3, qkv1, qkv2, qkv3,
-    send, recv, turn,
+    cos_t, sin_t, mask, send, recv, turn,
 ):
     sec = lax.axis_index("section")
     me = lax.axis_index("fsdp")
@@ -315,6 +315,7 @@
         g.start()
     low_x.start()
     high_z.start()
+
     for cp in to_rank:
         cp.wait_recv()
 
@@ -324,24 +325,39 @@
 
     gate_x.start()
     up_z.start()
+
+    row_no = lax.broadcasted_iota(jnp.int32, (TOK, TOK), 0)
+    col_no = lax.broadcasted_iota(jnp.int32, (TOK, TOK), 1)
+    seg_j = jnp.broadcast_to(seg[...].astype(F32), (TOK, TOK))
+    seg_i = seg_j.T
+    same_block = jnp.where(row_no < ROWS, 0, 1) == jnp.where(col_no < ROWS, 0, 1)
+    earlier = jnp.sum(
+        jnp.where(same_block & (seg_j < seg_i), 1.0, 0.0), axis=1, keepdims=True)
+    place = jnp.where(row_no < ROWS, row_no, row_no - ROWS).astype(F32) - earlier
+    angles = place * freq[0:1]
+    cos_t[...] = jnp.cos(angles)
+    sin_t[...] = jnp.sin(angles) * freq[1:2]
+    mask[...] = jnp.where(same_block & (seg_j == seg_i) & (col_no <= row_no), 1.0, 0.0)
     for g, after in zip(att_0, att_1):
-        g.end()
-        after.start()
-    low_x.end()
-    high_z.end()
-    for g, after in zip(att_1, att_2):
         g.end()
         after.start()
     gate_x.end()
     gate_z.start()
     up_z.end()
     up_x.start()
+    for g, after in zip(att_1, att_2):
+        g.end()
+        after.start()
+    low_x.end()
+    high_z.end()
     low_z.start()
     high_x.start()
     for g in att_2:
         g.mid()
     gate_z.mid()
     up_x.mid()
+    low_z.mid()
+    high_x.mid()
 
     @pl.when(sec == 0)
     def _():
@@ -475,8 +491,6 @@
 
     gate_z.end()
     up_x.end()
-    low_z.mid()
-    high_x.mid()
     low_z.end()
     high_x.end()
 
@@ -740,13 +754,17 @@
         lo = (rows - hi.astype(F32)).astype(BF16)
         return dot(hi, move) + dot(lo, move)
 
-    od[...] = unpadded(jnp.concatenate([rlow_x.total(), rhigh_z.total()], axis=1))[0:76]
+    def by_row(ref, rows):
+        for r in range(ref.shape[0]):
+            ref[r] = rows[r : r + 1]
+
+    by_row(od, unpadded(jnp.concatenate([rlow_x.total(), rhigh_z.total()], axis=1)))
     total = unpadded(out_red[2].total())
-    oout[...] = total[0:14]
+    by_row(oout, total)
     ogm[...] = own_lanes(total, 14)[14:15, 0:14]
     for n in range(3):
         proj[0:16, pl.ds(384 * n, 384)] = qkv_red[2][n].total()
-    oqkv[...] = proj[0:14, :]
+    by_row(oqkv, proj[0:16, :])
     ob[...] = own_lanes(proj[0:16, :], 18)[14:15, 0:18]
     oga[...] = own_lanes(proj[0:16, pl.ds(0, DP)], 16)[15:16, 0:14]
     ogu[y] = w_gu[z, x, mine, :]
@@ -773,21 +791,11 @@
     return (np.arange(D)[:, None] == row[None, :]).astype(jnp.bfloat16)
 
 
-def tables(segments):
-    seg = segments.reshape(TOK // ROWS, ROWS)
-    earlier = jnp.sum((seg[:, None, :] < seg[:, :, None]).astype(jnp.int32), axis=2)
-    place = (jnp.arange(ROWS, dtype=jnp.int32)[None] - earlier).astype(F32).reshape(TOK)
+def frequencies():
     half = HD // 2
-    inverse = theta_base ** (-(jnp.arange(half, dtype=F32) * 2.0 / HD))
-    angles = place[:, None] * jnp.tile(inverse, 4)[None, :]
-    sign = jnp.where(jnp.arange(128) % HD < half, -1.0, 1.0).astype(F32)
-    index = jnp.arange(TOK)
-    allowed = (
-        (segments[:, None] == segments[None, :])
-        & (index[None, :] <= index[:, None])
-        & (index[None, :] // ROWS == index[:, None] // ROWS)
-    )
-    return jnp.cos(angles), jnp.sin(angles) * sign, allowed.astype(F32)
+    inverse = theta_base ** (-(np.arange(half, dtype=np.float64) * 2.0 / HD))
+    sign = np.where(np.arange(128) % HD < half, -1.0, 1.0)
+    return np.concatenate([np.tile(inverse, 4)[None], sign[None], np.zeros((6, 128))]).astype(np.float32)
 
 
 def by_rank(weight):
@@ -803,7 +811,6 @@
 def body(
     tokens, segments, cotangent, w_qkv, b_qkv, w_out, gain_attn, gain_mlp, w_gate, w_up, w_down
 ):
-    cos_t, sin_t, mask = tables(segments)
     gu_in = jnp.concatenate([by_rank(w_gate[0]), by_rank(w_up[0])], axis=2)
     vec = jnp.concatenate(
         [jnp.pad(v, ((0, 0), (0, 128 - v.shape[1]))) for v in (b_qkv, gain_attn, gain_mlp)])
@@ -814,10 +821,10 @@
         kernel,
         out_shape=(
             sds((TOK, D), BF16), sds((TOK, D), F32), sds((4, 16, 2 * FP), BF16),
-            sds((76, D), F32), sds((14, QKV), F32), sds((14, D), F32),
+            sds((76, 1, D), F32), sds((14, 1, QKV), F32), sds((14, 1, D), F32),
             sds((1, 18), F32), sds((1, 14), F32), sds((1, 14), F32),
         ),
-        in_specs=[pl.BlockSpec(memory_space=pltpu.VMEM)] * 11,
+        in_specs=[pl.BlockSpec(memory_space=pltpu.VMEM)] * 10,
         out_specs=tuple([pl.BlockSpec(memory_space=pltpu.VMEM)] * 9),
         scratch_shapes=[
             vm((4, 4, 4, 16, ATT), BF16), vm((4, 4, 64, 2 * FP), BF16), vm((4, 4, 80, DP), BF16),
@@ -835,6 +842,7 @@
             vm((2, 2, 4, 80, 256), BF16), vm((2, 2, 4, 80, 512), BF16), vm((2, 3, 80, 512), BF16),
             vm((3, 4, 4, 16, DP), BF16), vm((3, 4, 16, DP), BF16), vm((3, 16, DP), BF16),
             vm((3, 3, 4, 4, 16, 384), BF16), vm((3, 3, 4, 16, 384), BF16), vm((3, 3, 16, 384), BF16),
+            *[vm((TOK, TOK), F32)] * 3,
             pltpu.SemaphoreType.DMA((N_SEM,)), pltpu.SemaphoreType.DMA((N_SEM,)),
             pltpu.SemaphoreType.REGULAR,
         ],
@@ -845,12 +853,13 @@
             flops=15 * 10**9, bytes_accessed=10 * 2**20, transcendentals=2 * 10**6
         ),
     )(
-        tokens, cotangent, cos_t, sin_t, mask, gu_in, w_down[0], w_qkv[0], w_out[0], vec,
+        tokens, cotangent, segments[None], jnp.asarray(frequencies()), gu_in, w_down[0], w_qkv[0], w_out[0], vec,
         jnp.asarray(pad_matrix()),
     )
+    rows = lambda array: array.transpose(1, 0, 2)
     return (
-        states[None], igrads[None], oqkv[None], b_grad, oout[None], ga_grad, gm_grad,
-        from_rank(ogu[:, :, :FP]), from_rank(ogu[:, :, FP:]), od[None],
+        states[None], igrads[None], rows(oqkv), b_grad, rows(oout), ga_grad, gm_grad,
+        from_rank(ogu[:, :, :FP]), from_rank(ogu[:, :, FP:]), rows(od),
     )
 
 

time: 214 us -> 200 us (0.935)
  Pallas kernels: 190 us -> 183 us
  local copies, waits for them, and re-layouts: 18.2 us -> 14.2 us
  other arithmetic: 4.18 us -> 1.55 us
    pallas_call x1, Pallas kernels: 190 us -> 183 us  [body(): pl.pallas_call(kernel, out_shape=(sds((TOK, D), BF16), sds((TOK, D), F32)...]
    unnamed x20 -> x26, local copies, waits for them, and re-layouts: 8.02 us -> 4.98 us
where the time goes in v3:
time: 200 us
  Pallas kernels  183 us (92%)
  local copies, waits for them, and re-layouts  14.2 us (7%)
    pallas_call x1, Pallas kernels, body(): pl.pallas_call(kernel, out_shape=(sds((TOK, D), BF16), sds((TOK, D), F32)...  183 us
    unnamed x26, local copies, waits for them, and re-layouts  4.98 us

profile of v3, /device:TPU:0, one launch (start us, length us, event | category | flops | bytes accessed | tf_op | source)
XLA Modules:
  0.0 200.0 jit_solution(4165060387709930761)
XLA Ops:
  0.7 0.7 fusion.5
  1.4 0.6 pad.27.vec
  2.0 1.6 reshape_squeeze.6
  3.7 0.1 pad.22
  3.8 0.3 reshape.62
  4.1 0.7 reshape_squeeze.7
  5.0 0.3 reshape.63
  5.3 0.7 pad_maximum_fusion.gu_in
  6.0 183.3 %shard_map.204 = (bf16[128,896]{1,0:T(8,128)(2,1)}, f32[128,896]{1,0:T(8,128)}, bf16[4,16,2560]{2,1,0:T(8,128)(2,1)}, f32[76,1,896]{2,1,0:T(1,128)}, f32[14,1,11...) custom-call(bf16[128,896]{1,0:T(8,128)(2,1)} %tok.1, ...), custom_call_target="tpu_custom_call" | custom-call | flops 15000000512 | bytes 10485760 | tf_op jit(solution)/shard_map/pallas_call | solution.py:820
  189.3 1.0 fusion.6
  190.4 0.4 reshape.65
  190.8 0.3 copy.26
  191.1 1.5 reshape.67
  192.7 0.4 reshape.64
  193.2 0.3 copy.25
  193.5 1.5 reshape.66
  195.0 0.7 copy.39
  195.7 0.8 copy.40
  196.5 0.6 copy.41
  197.1 0.5 copy.42
  197.6 0.6 copy.43
  198.2 0.5 copy.44
  198.7 0.5 copy.45
  199.3 0.7 copy.46
  (23 shorter events, 0.4 us)
Async XLA Ops:
  0.6 3.4 %copy-start.3 = (bf16[1,14,4864]{2,1,0:T(8,128)(2,1)S(1)}, bf16[1,14,4864]{2,1,0:T(8,128)(2,1)}, u32[]{:S(2)}) copy-start(bf16[1,14,4864]{2,1,0:T(8,128)(2,1)} %param.22) | copy-start | bytes 408580
  191.1 3.9 %copy-start.2 = (bf16[128,896]{1,0:T(8,128)(2,1)S(1)}, bf16[128,896]{1,0:T(8,128)(2,1)}, u32[]{:S(2)}) copy-start(bf16[128,896]{1,0:T(8,128)(2,1)} %get-tuple-element.19) | copy-start | bytes 688132
  191.1 4.6 %copy-start = (f32[128,896]{1,0:T(8,128)S(1)}, f32[128,896]{1,0:T(8,128)}, u32[]{:S(2)}) copy-start(f32[128,896]{1,0:T(8,128)} %get-tuple-element.20) | copy-start | bytes 1376260
  193.1 3.4 %copy-start.4 = (f32[14,1,1152]{2,1,0:T(1,128)S(1)}, f32[14,1,1152]{2,1,0:T(1,128)}, u32[]{:S(2)}) copy-start(f32[14,1,1152]{2,1,0:T(1,128)} %get-tuple-element.21) | copy-start | bytes 193540
  193.1 4.0 %copy-start.8 = (f32[1,18]{1,0:T(1,128)S(1)}, f32[1,18]{1,0:T(1,128)}, u32[]{:S(2)}) copy-start(f32[1,18]{1,0:T(1,128)} %get-tuple-element.43) | copy-start | bytes 220
  193.1 4.5 %copy-start.5 = (f32[14,1,896]{2,1,0:T(1,128)S(1)}, f32[14,1,896]{2,1,0:T(1,128)}, u32[]{:S(2)}) copy-start(f32[14,1,896]{2,1,0:T(1,128)} %get-tuple-element.23) | copy-start | bytes 150532
  193.1 5.1 %copy-start.7 = (f32[1,14]{1,0:T(1,128)S(1)}, f32[1,14]{1,0:T(1,128)}, u32[]{:S(2)}) copy-start(f32[1,14]{1,0:T(1,128)} %get-tuple-element.45) | copy-start | bytes 172
  193.1 5.7 %copy-start.6 = (f32[1,14]{1,0:T(1,128)S(1)}, f32[1,14]{1,0:T(1,128)}, u32[]{:S(2)}) copy-start(f32[1,14]{1,0:T(1,128)} %get-tuple-element.46) | copy-start | bytes 172
  193.1 6.2 %copy-start.1 = (f32[76,1,896]{2,1,0:T(1,128)S(1)}, f32[76,1,896]{2,1,0:T(1,128)}, u32[]{:S(2)}) copy-start(f32[76,1,896]{2,1,0:T(1,128)} %get-tuple-element.27) | copy-start | bytes 817156

commit v4 on v3

--- a/solution.py
+++ b/solution.py
@@ -717,12 +717,12 @@
 
     rlow_z.mid()
     rhigh_x.mid()
-    out_red[0].end()
-    out_red[1].start()
     rgate_z.end()
     rgate_x.start()
     rup_x.end()
     rup_z.start()
+    out_red[0].end()
+    out_red[1].start()
     for red, after in zip(qkv_red[0], qkv_red[1]):
         red.end()
         after.start()
@@ -813,8 +813,8 @@
 ):
     gu_in = jnp.concatenate([by_rank(w_gate[0]), by_rank(w_up[0])], axis=2)
     vec = jnp.concatenate(
-        [jnp.pad(v, ((0, 0), (0, 128 - v.shape[1]))) for v in (b_qkv, gain_attn, gain_mlp)])
-    vec = jnp.pad(vec, ((0, 13), (0, 0)))
+        [jnp.pad(v, ((0, 0), (0, 128 - v.shape[1]))) for v in (b_qkv, gain_attn, gain_mlp)]
+        + [jnp.zeros((13, 128), BF16)])
     sds = jax.ShapeDtypeStruct
     vm = pltpu.VMEM
     states, igrads, ogu, od, oqkv, oout, b_grad, ga_grad, gm_grad = pl.pallas_call(

time: 200 us -> 200 us (level)
  no operation moved by 1% of the time
where the time goes in v4:
time: 200 us
  Pallas kernels  183 us (92%)
  local copies, waits for them, and re-layouts  13.7 us (7%)
  other arithmetic  2.17 us (1%)
    pallas_call x1, Pallas kernels, body(): pl.pallas_call(kernel, out_shape=(sds((TOK, D), BF16), sds((TOK, D), F32)...  183 us
    unnamed x26, local copies, waits for them, and re-layouts  4.98 us

profile of v4, /device:TPU:0, one launch (start us, length us, event | category | flops | bytes accessed | tf_op | source)
XLA Modules:
  0.0 200.1 jit_solution(12387161535532529644)
XLA Ops:
  0.7 1.4 fusion.6.vec
  2.1 1.6 reshape_squeeze.6
  3.8 0.1 pad.18
  3.9 0.3 reshape.62
  4.2 0.7 reshape_squeeze.7
  5.0 0.1 pad.19
  5.1 0.3 reshape.63
  5.4 0.7 pad_maximum_fusion.gu_in
  6.1 183.4 %shard_map.204 = (bf16[128,896]{1,0:T(8,128)(2,1)}, f32[128,896]{1,0:T(8,128)}, bf16[4,16,2560]{2,1,0:T(8,128)(2,1)}, f32[76,1,896]{2,1,0:T(1,128)}, f32[14,1,11...) custom-call(bf16[128,896]{1,0:T(8,128)(2,1)} %tok.1, ...), custom_call_target="tpu_custom_call" | custom-call | flops 15000000512 | bytes 10485760 | tf_op jit(solution)/shard_map/pallas_call | solution.py:820
  189.5 1.0 fusion.8
  190.5 0.4 reshape.65
  190.9 0.3 copy.26
  191.3 1.5 reshape.67
  192.8 0.4 reshape.64
  193.3 0.3 copy.25
  193.6 1.5 reshape.66
  195.1 0.7 copy.39
  195.8 0.8 copy.40
  196.6 0.6 copy.41
  197.2 0.5 copy.42
  197.7 0.6 copy.43
  198.4 0.5 copy.44
  198.9 0.5 copy.45
  199.4 0.7 copy.46
  (24 shorter events, 0.4 us)
Async XLA Ops:
  0.6 3.5 %copy-start.3 = (bf16[1,14,4864]{2,1,0:T(8,128)(2,1)S(1)}, bf16[1,14,4864]{2,1,0:T(8,128)(2,1)}, u32[]{:S(2)}) copy-start(bf16[1,14,4864]{2,1,0:T(8,128)(2,1)} %param.22) | copy-start | bytes 408580
  191.2 3.9 %copy-start.2 = (bf16[128,896]{1,0:T(8,128)(2,1)S(1)}, bf16[128,896]{1,0:T(8,128)(2,1)}, u32[]{:S(2)}) copy-start(bf16[128,896]{1,0:T(8,128)(2,1)} %get-tuple-element.19) | copy-start | bytes 688132
  191.2 4.6 %copy-start = (f32[128,896]{1,0:T(8,128)S(1)}, f32[128,896]{1,0:T(8,128)}, u32[]{:S(2)}) copy-start(f32[128,896]{1,0:T(8,128)} %get-tuple-element.20) | copy-start | bytes 1376260
  193.2 3.4 %copy-start.4 = (f32[14,1,1152]{2,1,0:T(1,128)S(1)}, f32[14,1,1152]{2,1,0:T(1,128)}, u32[]{:S(2)}) copy-start(f32[14,1,1152]{2,1,0:T(1,128)} %get-tuple-element.21) | copy-start | bytes 193540
  193.2 4.0 %copy-start.8 = (f32[1,18]{1,0:T(1,128)S(1)}, f32[1,18]{1,0:T(1,128)}, u32[]{:S(2)}) copy-start(f32[1,18]{1,0:T(1,128)} %get-tuple-element.43) | copy-start | bytes 220
  193.2 4.5 %copy-start.5 = (f32[14,1,896]{2,1,0:T(1,128)S(1)}, f32[14,1,896]{2,1,0:T(1,128)}, u32[]{:S(2)}) copy-start(f32[14,1,896]{2,1,0:T(1,128)} %get-tuple-element.23) | copy-start | bytes 150532
  193.2 5.1 %copy-start.7 = (f32[1,14]{1,0:T(1,128)S(1)}, f32[1,14]{1,0:T(1,128)}, u32[]{:S(2)}) copy-start(f32[1,14]{1,0:T(1,128)} %get-tuple-element.45) | copy-start | bytes 172
  193.2 5.7 %copy-start.6 = (f32[1,14]{1,0:T(1,128)S(1)}, f32[1,14]{1,0:T(1,128)}, u32[]{:S(2)}) copy-start(f32[1,14]{1,0:T(1,128)} %get-tuple-element.46) | copy-start | bytes 172
  193.2 6.2 %copy-start.1 = (f32[76,1,896]{2,1,0:T(1,128)S(1)}, f32[76,1,896]{2,1,0:T(1,128)}, u32[]{:S(2)}) copy-start(f32[76,1,896]{2,1,0:T(1,128)} %get-tuple-element.27) | copy-start | bytes 817156

commit v5 on v4

--- a/solution.py
+++ b/solution.py
@@ -77,7 +77,7 @@
 
 def kernel(
     tok, cot, seg, freq, gu_in, d_in, qkv_in, out_in, vec, pad_s,
-    states, igrads, ogu, od, oqkv, oout, ob, oga, ogm,
+    states, igrads, ogate, oup, od, oqkv, oout, ob, oga, ogm,
     w_att, w_gu, w_d, g_out, g_qkv,
     xin, dyin, ybuf, dxbuf, h1, obuf, do_buf, datt, dp_buf, h1t, ot,
     h2all, dmall, gact, aact, dgu, h2t, at,
@@ -464,7 +464,7 @@
         return part[0].astype(F32) + (
             sums[0].astype(F32) + sums[1].astype(F32) + sums[2].astype(F32))
 
-    def mlp(k, n):
+    def mlp(k, n, need=()):
         rows = n * TOK
         for i in range(5):
             cols, cols_up = pl.ds(256 * i, 256), pl.ds(FP + 256 * i, 256)
@@ -475,6 +475,8 @@
             gact[k : k + n, :, cols_up] = upward.reshape(n, TOK, 256)
             aact[k : k + n, :, cols] = (
                 gate * jax.nn.sigmoid(gate) * upward).astype(BF16).reshape(n, TOK, 256)
+        for weights in need:
+            weights.end()
         for i in range(4):
             cols = pl.ds(256 * i, 256)
             a = aact[k : k + n].reshape(rows, FP)
@@ -491,10 +493,8 @@
 
     gate_z.end()
     up_x.end()
-    low_z.end()
-    high_x.end()
-
-    mlp(0, 1)
+
+    mlp(0, 1, (low_z, high_x))
     ag.mid()
     mlp(1, 2)
     go(sums[0])
@@ -767,11 +767,13 @@
     by_row(oqkv, proj[0:16, :])
     ob[...] = own_lanes(proj[0:16, :], 18)[14:15, 0:18]
     oga[...] = own_lanes(proj[0:16, pl.ds(0, DP)], 16)[15:16, 0:14]
-    ogu[y] = w_gu[z, x, mine, :]
+    ogate[y] = w_gu[z, x, mine, pl.ds(0, FP)]
+    oup[y] = w_gu[z, x, mine, pl.ds(FP, FP)]
     for cp in from_rank:
         cp.wait_recv()
     for step in (up1, up3, up2):
-        ogu[step(y)] = gu4[step(y)]
+        ogate[step(y)] = gu4[step(y), :, pl.ds(0, FP)]
+        oup[step(y)] = gu4[step(y), :, pl.ds(FP, FP)]
 
     for cp in pending + late:
         cp.wait_send()
@@ -817,15 +819,15 @@
         + [jnp.zeros((13, 128), BF16)])
     sds = jax.ShapeDtypeStruct
     vm = pltpu.VMEM
-    states, igrads, ogu, od, oqkv, oout, b_grad, ga_grad, gm_grad = pl.pallas_call(
+    states, igrads, ogate, oup, od, oqkv, oout, b_grad, ga_grad, gm_grad = pl.pallas_call(
         kernel,
         out_shape=(
-            sds((TOK, D), BF16), sds((TOK, D), F32), sds((4, 16, 2 * FP), BF16),
+            sds((TOK, D), BF16), sds((TOK, D), F32), sds((4, 16, FP), BF16), sds((4, 16, FP), BF16),
             sds((76, 1, D), F32), sds((14, 1, QKV), F32), sds((14, 1, D), F32),
             sds((1, 18), F32), sds((1, 14), F32), sds((1, 14), F32),
         ),
         in_specs=[pl.BlockSpec(memory_space=pltpu.VMEM)] * 10,
-        out_specs=tuple([pl.BlockSpec(memory_space=pltpu.VMEM)] * 9),
+        out_specs=tuple([pl.BlockSpec(memory_space=pltpu.VMEM)] * 10),
         scratch_shapes=[
             vm((4, 4, 4, 16, ATT), BF16), vm((4, 4, 64, 2 * FP), BF16), vm((4, 4, 80, DP), BF16),
             vm((4, 4, 4, 16, DP), BF16), vm((4, 4, 4, 16, QKV), BF16),
@@ -859,7 +861,7 @@
     rows = lambda array: array.transpose(1, 0, 2)
     return (
         states[None], igrads[None], rows(oqkv), b_grad, rows(oout), ga_grad, gm_grad,
-        from_rank(ogu[:, :, :FP]), from_rank(ogu[:, :, FP:]), rows(od),
+        from_rank(ogate), from_rank(oup), rows(od),
     )
 
 

time: 200 us -> 200 us (level)
    unnamed x26 -> x28, local copies, waits for them, and re-layouts: 4.98 us -> 4.98 us
where the time goes in v5:
time: 200 us
  Pallas kernels  183 us (92%)
  local copies, waits for them, and re-layouts  13.7 us (7%)
  other arithmetic  2.17 us (1%)
    pallas_call x1, Pallas kernels, body(): pl.pallas_call(kernel, out_shape=(sds((TOK, D), BF16), sds((TOK, D), F32)...  183 us
    unnamed x28, local copies, waits for them, and re-layouts  4.98 us

profile of v5, /device:TPU:0, one launch (start us, length us, event | category | flops | bytes accessed | tf_op | source)
XLA Modules:
  0.0 200.0 jit_solution(4667245922825970702)
XLA Ops:
  0.7 1.4 fusion.6.vec
  2.1 1.6 reshape_squeeze.6
  3.7 0.1 copy.30
  3.8 0.1 pad.18
  3.9 0.3 reshape.62
  4.2 0.7 reshape_squeeze.7
  5.0 0.1 pad.19
  5.1 0.3 reshape.63
  5.4 0.7 pad_maximum_fusion.gu_in
  6.1 183.3 %shard_map.204 = (bf16[128,896]{1,0:T(8,128)(2,1)}, f32[128,896]{1,0:T(8,128)}, bf16[4,16,1280]{2,1,0:T(8,128)(2,1)}, bf16[4,16,1280]{2,1,0:T(8,128)(2,1)}, f32[...) custom-call(bf16[128,896]{1,0:T(8,128)(2,1)} %tok.1, ...), custom_call_target="tpu_custom_call" | custom-call | flops 15000000512 | bytes 10485760 | tf_op jit(solution)/shard_map/pallas_call | solution.py:822
  189.5 1.3 reshape.64
  190.9 0.3 copy.25
  191.2 1.5 reshape.66
  192.7 0.4 reshape.65
  193.2 0.3 copy.26
  193.5 1.5 reshape.67
  195.1 0.7 copy.39
  195.8 0.8 copy.40
  196.5 0.6 copy.41
  197.2 0.5 copy.42
  197.7 0.6 copy.43
  198.3 0.5 copy.44
  198.8 0.5 copy.45
  199.3 0.7 copy.46
  (25 shorter events, 0.3 us)
Async XLA Ops:
  0.6 3.5 %copy-start.4 = (bf16[1,14,4864]{2,1,0:T(8,128)(2,1)S(1)}, bf16[1,14,4864]{2,1,0:T(8,128)(2,1)}, u32[]{:S(2)}) copy-start(bf16[1,14,4864]{2,1,0:T(8,128)(2,1)} %param.22) | copy-start | bytes 408580
  189.5 3.3 %copy-start.3 = (bf16[4,16,1280]{2,1,0:T(8,128)(2,1)S(1)}, bf16[4,16,1280]{2,1,0:T(8,128)(2,1)}, u32[]{:S(2)}) copy-start(bf16[4,16,1280]{2,1,0:T(8,128)(2,1)} %get-tuple-element.28) | copy-start | bytes 491524
  191.2 3.9 %copy-start.2 = (bf16[128,896]{1,0:T(8,128)(2,1)S(1)}, bf16[128,896]{1,0:T(8,128)(2,1)}, u32[]{:S(2)}) copy-start(bf16[128,896]{1,0:T(8,128)(2,1)} %get-tuple-element.20) | copy-start | bytes 688132
  191.2 4.6 %copy-start = (f32[128,896]{1,0:T(8,128)S(1)}, f32[128,896]{1,0:T(8,128)}, u32[]{:S(2)}) copy-start(f32[128,896]{1,0:T(8,128)} %get-tuple-element.21) | copy-start | bytes 1376260
  193.1 3.4 %copy-start.5 = (f32[14,1,1152]{2,1,0:T(1,128)S(1)}, f32[14,1,1152]{2,1,0:T(1,128)}, u32[]{:S(2)}) copy-start(f32[14,1,1152]{2,1,0:T(1,128)} %get-tuple-element.22) | copy-start | bytes 193540
  193.1 4.0 %copy-start.9 = (f32[1,18]{1,0:T(1,128)S(1)}, f32[1,18]{1,0:T(1,128)}, u32[]{:S(2)}) copy-start(f32[1,18]{1,0:T(1,128)} %get-tuple-element.43) | copy-start | bytes 220
  193.1 4.5 %copy-start.6 = (f32[14,1,896]{2,1,0:T(1,128)S(1)}, f32[14,1,896]{2,1,0:T(1,128)}, u32[]{:S(2)}) copy-start(f32[14,1,896]{2,1,0:T(1,128)} %get-tuple-element.24) | copy-start | bytes 150532
  193.2 5.1 %copy-start.8 = (f32[1,14]{1,0:T(1,128)S(1)}, f32[1,14]{1,0:T(1,128)}, u32[]{:S(2)}) copy-start(f32[1,14]{1,0:T(1,128)} %get-tuple-element.45) | copy-start | bytes 172
  193.2 5.7 %copy-start.7 = (f32[1,14]{1,0:T(1,128)S(1)}, f32[1,14]{1,0:T(1,128)}, u32[]{:S(2)}) copy-start(f32[1,14]{1,0:T(1,128)} %get-tuple-element.46) | copy-start | bytes 172
  193.2 6.2 %copy-start.1 = (f32[76,1,896]{2,1,0:T(1,128)S(1)}, f32[76,1,896]{2,1,0:T(1,128)}, u32[]{:S(2)}) copy-start(f32[76,1,896]{2,1,0:T(1,128)} %get-tuple-element.29) | copy-start | bytes 817156
